TPU v7x, 32 devices: a whole 2x2x4 slice. The times are simulated.
32 devices in a mesh: groups: 2 (over y), cube: 4 (over z), row: 2 (over x), pair: 2 (over core).
Axes of the slice: x: 2, y: 2, z: 4, core: 2. Of those that a mesh axis runs over, the one named last changes fastest.
Arguments:
- ligand: float32 [2, 64, 32, 1024], P('pair', ('groups', 'cube', 'row')), parts along dimension 1, may hold values from 0.05 to 3
- density: int32 [64, 32, 1024], P(('groups', 'cube', 'row')), parts along dimension 0, may hold values from 0 to 7
- counts: int32 [16], P(('groups', 'cube', 'row')), parts along dimension 0, may hold values from 1 to 4, as said below
- neighbours: int32 [64, 6], P(('groups', 'cube', 'row')), parts along dimension 0, may hold values from -1 to 31, as said below
- diffusion: float32 [2], replicated, may hold values from 0.04 to 0.14
- uptake: float32 [2], replicated, may hold values from 0.03 to 0.18
Outputs:
- ligand_out: float32 [2, 64, 32, 1024], P('pair', ('groups', 'cube', 'row')), parts along dimension 1
There are 2 independent parts, one for each index of `groups`. A program takes and returns all parts, laid end to end along the dimension named above; an argument that names none is the same for every part. Nothing has to cross between parts.
Inputs may be any that keep to these rules, and one draw needn't show every extreme that they name: `counts`: the number of occupied tiles of each block of 4 slots; they fill the first slots of their block; some block is full and some block holds 1. Block b = layer * 2 + band holds tile slots b * 4 to (b + 1) * 4 - 1; an entry is -1 for an empty slot, for a face on the volume's boundary and for an unoccupied place; x neighbours lie in the same block, a -y neighbour in block b or b - 1, a +y neighbour in block b or b + 1, a -z neighbour in block b - 2, a +z neighbour in block b + 2; if tile u names v across a face, v names u across the opposite face.
All inputs are finite; a program needn't handle non-finite values.
Results may differ from a plain program's by a relative error of at most 0.00007.
Values sent between devices are 32-bit elements; how exact they have to be, the bound alone decides.
A program may use at most 64 MiB of HBM per device.

v0:
```python
import functools

import jax
import jax.numpy as jnp
from jax import lax
from jax.experimental import pallas as pl
from jax.experimental.pallas import tpu as pltpu
from jax.sharding import PartitionSpec as P

EY = 32
STEPS = 4
LANES = 128
ROWS = 8
MESH = pl.DeviceIdType.MESH


def kernel(
    layers, bands, slots, half, cells,
    nbr, counts, diffusion, uptake, ligand, density, out,
    field, dens, stage, y_high, y_low, y_minus, y_plus, z_low, z_high, z_minus, z_plus,
    extra, y_first, y_here, z_first_low, z_first_high, first_send, first_recv,
    load_sem, swap_send, swap_recv, face_send, face_recv, out_send, out_recv,
):
    core = lax.axis_index("pair")
    layer = lax.axis_index("cube")
    band = lax.axis_index("row")
    block = layer * bands + band
    other = 1 - core
    columns = cells // LANES
    has_minus = band > 0
    has_plus = band < bands - 1
    far_layer = jnp.where(core == 0, layer - 1, layer + 1)
    has_far = jnp.logical_and(far_layer >= 0, far_layer < layers)
    partner_id = {"pair": other}
    far_id = {"cube": far_layer, "pair": other}
    minus_id = {"row": band - 1}
    plus_id = {"row": band + 1}

    own_rows = pl.ds(pl.multiple_of(core * half, half), half)
    other_rows = pl.ds(pl.multiple_of(other * half, half), half)
    loads = [
        pltpu.make_async_copy(ligand.at[0, :, own_rows, :], field.at[0, core], load_sem.at[0]),
        pltpu.make_async_copy(ligand.at[0, :, other_rows, :], extra, load_sem.at[2]),
        pltpu.make_async_copy(density.at[:, own_rows, :], dens, load_sem.at[1]),
    ]
    for load in loads:
        load.start()

    barrier = pltpu.get_barrier_semaphore()
    has_down = layer > 0
    has_up = layer < layers - 1
    always = layer >= 0
    greeted = [
        (always, partner_id),
        (has_far, far_id),
        (has_down, {"cube": layer - 1}),
        (has_up, {"cube": layer + 1}),
        (has_minus, minus_id),
        (has_plus, plus_id),
        (has_minus, {"row": band - 1, "pair": other}),
        (has_plus, {"row": band + 1, "pair": other}),
    ]
    peers = jnp.int32(0)
    for wanted, device in greeted:
        pl.when(wanted)(
            functools.partial(
                pl.semaphore_signal, barrier, inc=1, device_id=device, device_id_type=MESH
            )
        )
        peers = peers + wanted.astype(jnp.int32)
    pl.semaphore_wait(barrier, peers)

    swap = pltpu.make_async_remote_copy(
        src_ref=ligand.at[0, :, other_rows, :], dst_ref=field.at[0, core],
        send_sem=swap_send, recv_sem=swap_recv, device_id=partner_id, device_id_type=MESH,
    )
    swap_in = pltpu.make_async_remote_copy(
        src_ref=ligand.at[0, :, other_rows, :], dst_ref=field.at[0, other],
        send_sem=swap_send, recv_sem=swap_recv, device_id=partner_id, device_id_type=MESH,
    )
    swap.start()

    def remote(source, target, step, k, device):
        return pltpu.make_async_remote_copy(
            src_ref=source.at[step], dst_ref=target[step],
            send_sem=face_send.at[step, k], recv_sem=face_recv.at[step, k],
            device_id=device, device_id_type=MESH,
        )

    def messages(step):
        first, last = core == 0, core == 1
        up_far = remote(z_high, z_minus, step, 0, far_id)
        up_near = remote(z_high, z_minus, step, 0, partner_id)
        down_far = remote(z_low, z_plus, step, 1, far_id)
        down_near = remote(z_low, z_plus, step, 1, partner_id)
        to_plus = remote(y_high, y_minus, step, 2, plus_id)
        to_minus = remote(y_low, y_plus, step, 3, minus_id)
        both = jnp.logical_and
        sends = [
            (has_plus, to_plus), (has_minus, to_minus),
            (both(last, has_far), up_far), (both(first, has_far), down_far),
            (first, up_near), (last, down_near),
        ]
        receives = [
            (jnp.logical_or(last, has_far), up_near), (jnp.logical_or(first, has_far), down_near),
            (has_minus, to_plus), (has_plus, to_minus),
        ]
        return sends, receives

    def first_copy(source, target, k, at, device):
        return pltpu.make_async_remote_copy(
            src_ref=source, dst_ref=target.at[core],
            send_sem=first_send.at[k], recv_sem=first_recv.at[at, core],
            device_id=device, device_id_type=MESH,
        )

    def first_sends():
        return [
            (core == 0, first_copy(z_first_high.at[0], z_minus[0], 0, 0, partner_id)),
            (core == 1, first_copy(z_first_low.at[1], z_plus[0], 1, 1, partner_id)),
            (has_down, first_copy(
                z_first_low.at[0], z_plus[0], 2, 1, {"cube": layer - 1, "pair": core * 0 + 1})),
            (has_up, first_copy(
                z_first_high.at[1], z_minus[0], 3, 0, {"cube": layer + 1, "pair": core * 0})),
        ] + [
            (has_plus, first_copy(
                y_first.at[h], y_minus[0], 4 + h, 2, {"row": band + 1, "pair": core * 0 + h}))
            for h in range(2)
        ] + [
            (has_minus, first_copy(
                y_first.at[h], y_plus[0], 6 + h, 3, {"row": band - 1, "pair": core * 0 + h}))
            for h in range(2)
        ]

    def arrived(target, at, species):
        pltpu.make_async_remote_copy(
            src_ref=target.at[species], dst_ref=target.at[species],
            send_sem=first_send.at[0], recv_sem=first_recv.at[at, species],
            device_id=partner_id, device_id_type=MESH,
        ).wait_recv()

    def wait_first():
        both, either = jnp.logical_and, jnp.logical_or
        for species in range(2):
            across = core == 1 - species
            minus = either(both(core == 0, has_down), both(core == 1, across))
            plus = either(both(core == 1, has_up), both(core == 0, across))
            pl.when(minus)(functools.partial(arrived, z_minus[0], 0, species))
            pl.when(plus)(functools.partial(arrived, z_plus[0], 1, species))
            pl.when(has_minus)(functools.partial(arrived, y_minus[0], 2, species))
            pl.when(has_plus)(functools.partial(arrived, y_plus[0], 3, species))

    def send_faces(step):
        for wanted, copy in messages(step)[0]:
            pl.when(wanted)(copy.start)

    def wait_faces(step):
        for wanted, copy in messages(step)[1]:
            pl.when(wanted)(copy.wait_recv)

    def wait_sent(step):
        for wanted, copy in messages(step)[0]:
            pl.when(wanted)(copy.wait_send)

    lane = lax.broadcasted_iota(jnp.int32, (ROWS, LANES), 1)
    pair_of = lax.rem(lane + 1, EY) // 2
    even = lax.rem(lane, 2) == 0
    wide = lax.broadcasted_iota(jnp.int32, (half, LANES), 1)
    at_low = lax.rem(wide, EY) == 0
    at_high = lax.rem(wide, EY) == EY - 1
    at_edge = jnp.logical_or(at_low, at_high)
    below_32 = wide < EY
    above_96 = wide >= LANES - EY

    def roll(value, shift):
        shift = shift % LANES
        return value if shift == 0 else pltpu.roll(value, shift, axis=1)

    pieces = [(zv, j) for zv in range(half // ROWS) for j in range(columns)]

    def pack(parts):
        total = None
        for m, (zv, j) in enumerate(pieces):
            piece = roll(parts[j][zv * ROWS : (zv + 1) * ROWS], 2 * m)
            total = piece if total is None else jnp.where(pair_of == m, piece, total)
        return total

    def put_faces(step, tile, both):
        packed = []
        for species in range(2):
            parts = both[species]
            packed.append(pack(parts))
            for j in range(columns):
                at = slice(j * LANES, (j + 1) * LANES)
                z_low[step, species, tile, :, at] = parts[j][:1]
                z_high[step, species, tile, :, at] = parts[j][half - 1 :]
        second = roll(packed[1], 1)
        y_low[step, tile] = jnp.where(even, packed[0], second)
        y_high[step, tile] = jnp.where(even, second, packed[0])

    def columns_of(value):
        return [value[:, j * LANES : (j + 1) * LANES] for j in range(columns)]

    def first_faces(tile, carry):
        for h, value in ((core, field[0, core, tile]), (other, extra[tile])):
            packed = pack(columns_of(value))
            y_first[h, tile] = packed
            z_first_low[h, tile] = value[:1]
            z_first_high[h, tile] = value[half - 1 :]
            if h is core:
                y_here[core, tile] = packed
        return carry

    def other_faces(tile, carry):
        y_here[other, tile] = pack(columns_of(field[0, other, tile]))
        return carry

    def own_planes():
        @pl.when(core == 0)
        def _():
            z_plus[0][0] = z_first_low[1]

        @pl.when(core == 1)
        def _():
            z_minus[0][1] = z_first_high[0]

    zero = jnp.float32(0.0)
    row = lax.broadcasted_iota(jnp.int32, (half, LANES), 0)

    def entry(tile, k):
        value = nbr[tile, k]
        safe = jnp.maximum(value, 0)
        return value >= 0, lax.rem(safe, slots), safe // slots == block

    def inner(step, tile):
        now, later = step % 2, (step + 1) % 2
        filled = tile < counts[0]
        left_ok, left, _ = entry(tile, 0)
        right_ok, right, _ = entry(tile, 1)
        fields = []
        for species in range(2):
            parts = columns_of(field[now, species, tile])
            if step == 0:
                parts = [jnp.where(filled, part, zero) for part in parts]
            fields.append(parts)
        amount = columns_of(dens[tile])
        share = [
            amount[j].astype(jnp.float32) / (1.0 + fields[0][j] + fields[1][j])
            for j in range(columns)
        ]
        blank = jnp.zeros((1, LANES), jnp.float32)
        for species in range(2):
            parts = fields[species]
            rate = diffusion[species]
            keep = 1.0 - 6.0 * rate
            taken = uptake[species] * 0.125
            ghost_left = roll(field[now, species, left, :, cells - LANES :], EY)
            ghost_right = roll(field[now, species, right, :, :LANES], -EY)
            forward = [jnp.where(left_ok, ghost_left, zero)] + [roll(part, EY) for part in parts]
            backward = [roll(part, -EY) for part in parts] + [jnp.where(right_ok, ghost_right, zero)]
            for j in range(columns):
                part = parts[j]
                value = jnp.where(below_32, forward[j], forward[j + 1])
                value = value + jnp.where(above_96, backward[j + 1], backward[j])
                value = value + jnp.where(at_low, zero, roll(part, 1))
                value = value + jnp.where(at_high, zero, roll(part, -1))
                value = value + jnp.concatenate([blank, part[: half - 1]], axis=0)
                value = value + jnp.concatenate([part[1:], blank], axis=0)
                at = slice(j * LANES, (j + 1) * LANES)
                field[later, species, tile, :, at] = (
                    part * (keep - taken * share[j]) + rate * value
                )

    def outer(step, tile):
        later = (step + 1) % 2
        filled = tile < counts[0]
        front_ok, front, front_here = entry(tile, 2)
        back_ok, back, back_here = entry(tile, 3)
        lower_ok, lower, _ = entry(tile, 4)
        upper_ok, upper, _ = entry(tile, 5)
        first = core == 0
        lower = jnp.where(first, lower, tile)
        lower_ok = jnp.where(first, lower_ok, filled)
        upper = jnp.where(first, tile, upper)
        upper_ok = jnp.where(first, filled, upper_ok)
        result = []
        for species in range(2):
            rate = diffusion[species]
            if step == 0:
                shift = 0
                from_front = jnp.where(front_here, y_here[species, front], y_minus[0][species, front])
                from_back = jnp.where(back_here, y_here[species, back], y_plus[0][species, back])
            else:
                shift = species
                from_front = jnp.where(front_here, y_high[step, front], y_minus[step][front])
                from_back = jnp.where(back_here, y_low[step, back], y_plus[step][back])
            from_front = jnp.where(front_ok, from_front, zero)
            from_back = jnp.where(back_ok, from_back, zero)
            ghost_y = rate * jnp.where(
                even, roll(from_front, 1 - EY - shift), roll(from_back, EY - 1 - shift)
            )
            below = rate * jnp.where(lower_ok, z_minus[step][species, lower], zero)
            above = rate * jnp.where(upper_ok, z_plus[step][species, upper], zero)
            values = []
            for j in range(columns):
                at = slice(j * LANES, (j + 1) * LANES)
                edge = jnp.concatenate(
                    [roll(ghost_y, -2 * (zv * columns + j)) for zv in range(half // ROWS)], axis=0
                )
                value = field[later, species, tile, :, at] + jnp.where(at_edge, edge, zero)
                value = value + jnp.where(row == 0, below[:, at], zero)
                value = value + jnp.where(row == half - 1, above[:, at], zero)
                values.append(value)
            result.append(values)
        return result

    def inner_step(step):
        def body(tile, carry):
            inner(step, tile)
            return carry

        lax.fori_loop(0, slots, body, 0)

    def outer_step(step):
        later = (step + 1) % 2

        def body(tile, carry):
            result = outer(step, tile)
            for species in range(2):
                for j in range(columns):
                    at = slice(j * LANES, (j + 1) * LANES)
                    field[later, species, tile, :, at] = result[species][j]
            put_faces(step + 1, tile, result)
            return carry

        lax.fori_loop(0, slots, body, 0, unroll=True)

    def give(tile):
        return pltpu.make_async_remote_copy(
            src_ref=stage.at[tile], dst_ref=out.at[0, tile, own_rows, :],
            send_sem=out_send.at[tile], recv_sem=out_recv.at[tile],
            device_id=partner_id, device_id_type=MESH,
        )

    def take(tile):
        return pltpu.make_async_remote_copy(
            src_ref=stage.at[tile], dst_ref=out.at[0, tile, other_rows, :],
            send_sem=out_send.at[tile], recv_sem=out_recv.at[tile],
            device_id=partner_id, device_id_type=MESH,
        )

    loads[0].wait()
    loads[1].wait()
    lax.fori_loop(0, slots, first_faces, 0, unroll=True)
    for wanted, copy in first_sends():
        pl.when(wanted)(copy.start)
    own_planes()
    loads[2].wait()
    swap_in.wait_recv()
    lax.fori_loop(0, slots, other_faces, 0, unroll=True)
    for step in range(STEPS):
        inner_step(step)
        if step == 0:
            wait_first()
        else:
            wait_faces(step)
        if step < STEPS - 1:
            outer_step(step)
            send_faces(step + 1)

    def last_body(tile, carry):
        result = outer(STEPS - 1, tile)
        for j in range(columns):
            at = slice(j * LANES, (j + 1) * LANES)
            stage[tile, :, at] = jnp.where(core == 0, result[1][j], result[0][j])
        give(tile).start()
        for j in range(columns):
            at = slice(j * LANES, (j + 1) * LANES)
            out[0, tile, own_rows, at] = jnp.where(core == 0, result[0][j], result[1][j])
        return carry

    lax.fori_loop(0, slots, last_body, 0, unroll=True)
    swap.wait_send()
    for wanted, copy in first_sends():
        pl.when(wanted)(copy.wait_send)
    for step in range(1, STEPS):
        wait_sent(step)
    for tile in range(slots):
        give(tile).wait_send()
        take(tile).wait_recv()


def per_device(layers, bands, ligand, density, counts, neighbours, diffusion, uptake):
    _, slots, depth, cells = ligand.shape
    half = depth // 2
    faces = (slots, ROWS, LANES)
    planes = (2, slots, 1, cells)
    smem = pl.BlockSpec(memory_space=pltpu.SMEM)
    away = pl.BlockSpec(memory_space=pltpu.HBM)
    return pl.pallas_call(
        functools.partial(kernel, layers, bands, slots, half, cells),
        out_shape=jax.ShapeDtypeStruct(ligand.shape, jnp.float32),
        in_specs=[smem, smem, smem, smem, away, away],
        out_specs=pl.BlockSpec(memory_space=pltpu.VMEM),
        scratch_shapes=[
            pltpu.VMEM((2, 2, slots, half, cells), jnp.float32),
            pltpu.VMEM((slots, half, cells), jnp.int32),
            pltpu.VMEM((slots, half, cells), jnp.float32),
            pltpu.VMEM((STEPS,) + faces, jnp.float32),
            pltpu.VMEM((STEPS,) + faces, jnp.float32),
            [pltpu.VMEM((2,) + faces, jnp.float32)] + [pltpu.VMEM(faces, jnp.float32)] * (STEPS - 1),
            [pltpu.VMEM((2,) + faces, jnp.float32)] + [pltpu.VMEM(faces, jnp.float32)] * (STEPS - 1),
            pltpu.VMEM((STEPS,) + planes, jnp.float32),
            pltpu.VMEM((STEPS,) + planes, jnp.float32),
            [pltpu.VMEM(planes, jnp.float32)] * STEPS,
            [pltpu.VMEM(planes, jnp.float32)] * STEPS,
            pltpu.VMEM((slots, half, cells), jnp.float32),
            pltpu.VMEM((2,) + faces, jnp.float32),
            pltpu.VMEM((2,) + faces, jnp.float32),
            pltpu.VMEM(planes, jnp.float32),
            pltpu.VMEM(planes, jnp.float32),
            pltpu.SemaphoreType.DMA((8,)),
            pltpu.SemaphoreType.DMA((4, 2)),
            pltpu.SemaphoreType.DMA((3,)),
            pltpu.SemaphoreType.DMA,
            pltpu.SemaphoreType.DMA,
            pltpu.SemaphoreType.DMA((STEPS, 4)),
            pltpu.SemaphoreType.DMA((STEPS, 4)),
            pltpu.SemaphoreType.DMA((slots,)),
            pltpu.SemaphoreType.DMA((slots,)),
        ],
        compiler_params=pltpu.CompilerParams(
            collective_id=0, has_side_effects=True, vmem_limit_bytes=53 * 1024 * 1024
        ),
    )(neighbours, counts, diffusion, uptake, ligand, density)


def solution(mesh):
    in_specs = (
        P("pair", ("groups", "cube", "row"), None, None),
        P(("groups", "cube", "row"), None, None),
        P(("groups", "cube", "row")),
        P(("groups", "cube", "row"), None),
        P(),
        P(),
    )
    out_specs = P("pair", ("groups", "cube", "row"), None, None)
    return jax.shard_map(
        functools.partial(per_device, mesh.shape["cube"], mesh.shape["row"]),
        mesh=mesh, in_specs=in_specs, out_specs=out_specs, check_vma=False,
    )
```

profile of v0, /device:TPU:0, one launch (start us, length us, event | category | flops | bytes accessed | tf_op | source)
XLA Modules:
  0.0 21.4 jit_solution(1177733410883720034)
XLA Ops:
  0.0 0.0 copy-start.2
  0.0 0.0 copy-start.1
  0.7 0.0 copy-done.2
  0.7 0.0 copy-done.1
  0.7 0.0 copy-start
  0.7 0.7 %copy-done = s32[4,6]{1,0:T(4,128)S(1)} copy-done((s32[4,6]{1,0:T(4,128)S(1)}, s32[4,6]{1,0:T(4,128)}, u32[]{:S(2)}) %copy-start) | copy-done | bytes 120
  1.4 19.2 %shard_map.64 = f32[1,4,32,1024]{3,2,1,0:T(8,128)S(1)} custom-call(s32[4,6]{1,0:T(4,128)S(1)} %copy-done, s32[1]{0:T(128)S(6)} %copy.8.counts, f32[2]{0:T(128)S(1)} %copy-done.1, f32[2]{0:T(128)S(1)} %copy-done.2, f32[1,4,32,1024]{3,2,1,0:T(8,128)} %ligand.1, s32[4,32,1024]{2,1,0:T(8,128)} %density.1), custom_call_target="tpu_custom_call" | custom-call | tf_op jit(solution)/shard_map/pallas_call | solution.py:400
  20.6 0.8 %copy.9 = f32[1,4,32,1024]{3,2,1,0:T(8,128)} copy(f32[1,4,32,1024]{3,2,1,0:T(8,128)S(1)} %shard_map.64) | data formatting | bytes 1048576
Async XLA Ops:
  0.0 0.7 %copy-start.2 = (f32[2]{0:T(128)S(1)}, f32[2]{0:T(128)}, u32[]{:S(2)}) copy-start(f32[2]{0:T(128)} %uptake.1) | copy-start | bytes 28
  0.0 0.7 %copy-start.1 = (f32[2]{0:T(128)S(1)}, f32[2]{0:T(128)}, u32[]{:S(2)}) copy-start(f32[2]{0:T(128)} %diffusion.1) | copy-start | bytes 28
  0.7 0.7 %copy-start = (s32[4,6]{1,0:T(4,128)S(1)}, s32[4,6]{1,0:T(4,128)}, u32[]{:S(2)}) copy-start(s32[4,6]{1,0:T(4,128)} %nbr.1) | copy-start | bytes 292
where the time goes:
time: 21.6 us; the launch traced here: 21.4 us
  Pallas kernels  19.2 us (89%)
  local copies, waits for them, and re-layouts  1.48 us (7%)
  between operations  0.71 us (3%)
    pallas_call x1, Pallas kernels, per_device(): pl.pallas_call(functools.partial(kernel, layers, bands, slots, half, cell...  19.2 us
    unnamed x7, local copies, waits for them, and re-layouts  1.48 us

commit v1 on v0

--- a/solution.py
+++ b/solution.py
@@ -16,34 +16,45 @@
 
 def kernel(
     layers, bands, slots, half, cells,
-    nbr, counts, diffusion, uptake, ligand, density, out,
+    nbr_in, counts_in, diffusion_in, uptake_in, ligand, density, out,
     field, dens, stage, y_high, y_low, y_minus, y_plus, z_low, z_high, z_minus, z_plus,
-    extra, y_first, y_here, z_first_low, z_first_high, first_send, first_recv,
-    load_sem, swap_send, swap_recv, face_send, face_recv, out_send, out_recv,
+    extra, y_first, y_here, z_first_low, z_first_high, nbr, counts, diffusion, uptake,
+    first_send, first_recv,
+    load_sem, small_sem, swap_send, swap_recv, face_send, face_recv, out_send, out_recv,
 ):
     core = lax.axis_index("pair")
     layer = lax.axis_index("cube")
     band = lax.axis_index("row")
     block = layer * bands + band
     other = 1 - core
+    part = lax.rem(core + band, 2)
+    rest = 1 - part
+    low_core = lax.rem(band, 2)
+    high_core = 1 - low_core
     columns = cells // LANES
     has_minus = band > 0
     has_plus = band < bands - 1
-    far_layer = jnp.where(core == 0, layer - 1, layer + 1)
+    far_layer = jnp.where(part == 0, layer - 1, layer + 1)
     has_far = jnp.logical_and(far_layer >= 0, far_layer < layers)
     partner_id = {"pair": other}
     far_id = {"cube": far_layer, "pair": other}
-    minus_id = {"row": band - 1}
-    plus_id = {"row": band + 1}
-
-    own_rows = pl.ds(pl.multiple_of(core * half, half), half)
-    other_rows = pl.ds(pl.multiple_of(other * half, half), half)
+    minus_id = {"row": band - 1, "pair": other}
+    plus_id = {"row": band + 1, "pair": other}
+
+    own_rows = pl.ds(pl.multiple_of(part * half, half), half)
+    other_rows = pl.ds(pl.multiple_of(rest * half, half), half)
     loads = [
         pltpu.make_async_copy(ligand.at[0, :, own_rows, :], field.at[0, core], load_sem.at[0]),
         pltpu.make_async_copy(ligand.at[0, :, other_rows, :], extra, load_sem.at[2]),
         pltpu.make_async_copy(density.at[:, own_rows, :], dens, load_sem.at[1]),
     ]
-    for load in loads:
+    smalls = [
+        pltpu.make_async_copy(source, target, small_sem.at[k])
+        for k, (source, target) in enumerate(
+            [(nbr_in, nbr), (counts_in, counts), (diffusion_in, diffusion), (uptake_in, uptake)]
+        )
+    ]
+    for load in loads + smalls:
         load.start()
 
     barrier = pltpu.get_barrier_semaphore()
@@ -57,8 +68,8 @@
         (has_up, {"cube": layer + 1}),
         (has_minus, minus_id),
         (has_plus, plus_id),
-        (has_minus, {"row": band - 1, "pair": other}),
-        (has_plus, {"row": band + 1, "pair": other}),
+        (has_minus, {"row": band - 1}),
+        (has_plus, {"row": band + 1}),
     ]
     peers = jnp.int32(0)
     for wanted, device in greeted:
@@ -88,7 +99,7 @@
         )
 
     def messages(step):
-        first, last = core == 0, core == 1
+        first, last = part == 0, part == 1
         up_far = remote(z_high, z_minus, step, 0, far_id)
         up_near = remote(z_high, z_minus, step, 0, partner_id)
         down_far = remote(z_low, z_plus, step, 1, far_id)
@@ -116,19 +127,19 @@
 
     def first_sends():
         return [
-            (core == 0, first_copy(z_first_high.at[0], z_minus[0], 0, 0, partner_id)),
-            (core == 1, first_copy(z_first_low.at[1], z_plus[0], 1, 1, partner_id)),
+            (part == 0, first_copy(z_first_high.at[0], z_minus[0], 0, 0, partner_id)),
+            (part == 1, first_copy(z_first_low.at[1], z_plus[0], 1, 1, partner_id)),
             (has_down, first_copy(
-                z_first_low.at[0], z_plus[0], 2, 1, {"cube": layer - 1, "pair": core * 0 + 1})),
+                z_first_low.at[0], z_plus[0], 2, 1, {"cube": layer - 1, "pair": high_core})),
             (has_up, first_copy(
-                z_first_high.at[1], z_minus[0], 3, 0, {"cube": layer + 1, "pair": core * 0})),
+                z_first_high.at[1], z_minus[0], 3, 0, {"cube": layer + 1, "pair": low_core})),
         ] + [
             (has_plus, first_copy(
-                y_first.at[h], y_minus[0], 4 + h, 2, {"row": band + 1, "pair": core * 0 + h}))
+                y_first.at[h], y_minus[0], 4 + h, 2, {"row": band + 1, "pair": lax.rem(band + 1 + h, 2)}))
             for h in range(2)
         ] + [
             (has_minus, first_copy(
-                y_first.at[h], y_plus[0], 6 + h, 3, {"row": band - 1, "pair": core * 0 + h}))
+                y_first.at[h], y_plus[0], 6 + h, 3, {"row": band - 1, "pair": lax.rem(band + 1 + h, 2)}))
             for h in range(2)
         ]
 
@@ -143,8 +154,8 @@
         both, either = jnp.logical_and, jnp.logical_or
         for species in range(2):
             across = core == 1 - species
-            minus = either(both(core == 0, has_down), both(core == 1, across))
-            plus = either(both(core == 1, has_up), both(core == 0, across))
+            minus = either(both(part == 0, has_down), both(part == 1, across))
+            plus = either(both(part == 1, has_up), both(part == 0, across))
             pl.when(minus)(functools.partial(arrived, z_minus[0], 0, species))
             pl.when(plus)(functools.partial(arrived, z_plus[0], 1, species))
             pl.when(has_minus)(functools.partial(arrived, y_minus[0], 2, species))
@@ -202,12 +213,12 @@
         return [value[:, j * LANES : (j + 1) * LANES] for j in range(columns)]
 
     def first_faces(tile, carry):
-        for h, value in ((core, field[0, core, tile]), (other, extra[tile])):
+        for h, value in ((part, field[0, core, tile]), (rest, extra[tile])):
             packed = pack(columns_of(value))
             y_first[h, tile] = packed
             z_first_low[h, tile] = value[:1]
             z_first_high[h, tile] = value[half - 1 :]
-            if h is core:
+            if h is part:
                 y_here[core, tile] = packed
         return carry
 
@@ -216,13 +227,13 @@
         return carry
 
     def own_planes():
-        @pl.when(core == 0)
+        @pl.when(part == 0)
         def _():
-            z_plus[0][0] = z_first_low[1]
-
-        @pl.when(core == 1)
+            z_plus[0][core] = z_first_low[1]
+
+        @pl.when(part == 1)
         def _():
-            z_minus[0][1] = z_first_high[0]
+            z_minus[0][core] = z_first_high[0]
 
     zero = jnp.float32(0.0)
     row = lax.broadcasted_iota(jnp.int32, (half, LANES), 0)
@@ -278,7 +289,7 @@
         back_ok, back, back_here = entry(tile, 3)
         lower_ok, lower, _ = entry(tile, 4)
         upper_ok, upper, _ = entry(tile, 5)
-        first = core == 0
+        first = part == 0
         lower = jnp.where(first, lower, tile)
         lower_ok = jnp.where(first, lower_ok, filled)
         upper = jnp.where(first, tile, upper)
@@ -349,6 +360,8 @@
             device_id=partner_id, device_id_type=MESH,
         )
 
+    for load in smalls:
+        load.wait()
     loads[0].wait()
     loads[1].wait()
     lax.fori_loop(0, slots, first_faces, 0, unroll=True)
@@ -395,12 +408,11 @@
     half = depth // 2
     faces = (slots, ROWS, LANES)
     planes = (2, slots, 1, cells)
-    smem = pl.BlockSpec(memory_space=pltpu.SMEM)
     away = pl.BlockSpec(memory_space=pltpu.HBM)
     return pl.pallas_call(
         functools.partial(kernel, layers, bands, slots, half, cells),
         out_shape=jax.ShapeDtypeStruct(ligand.shape, jnp.float32),
-        in_specs=[smem, smem, smem, smem, away, away],
+        in_specs=[away] * 6,
         out_specs=pl.BlockSpec(memory_space=pltpu.VMEM),
         scratch_shapes=[
             pltpu.VMEM((2, 2, slots, half, cells), jnp.float32),
@@ -419,9 +431,14 @@
             pltpu.VMEM((2,) + faces, jnp.float32),
             pltpu.VMEM(planes, jnp.float32),
             pltpu.VMEM(planes, jnp.float32),
+            pltpu.SMEM((slots, 6), jnp.int32),
+            pltpu.SMEM((1,), jnp.int32),
+            pltpu.SMEM((2,), jnp.float32),
+            pltpu.SMEM((2,), jnp.float32),
             pltpu.SemaphoreType.DMA((8,)),
             pltpu.SemaphoreType.DMA((4, 2)),
             pltpu.SemaphoreType.DMA((3,)),
+            pltpu.SemaphoreType.DMA((4,)),
             pltpu.SemaphoreType.DMA,
             pltpu.SemaphoreType.DMA,
             pltpu.SemaphoreType.DMA((STEPS, 4)),

time: 21.6 us -> 20.5 us (0.949)
  Pallas kernels: 19.2 us -> 18.1 us
    pallas_call x1, Pallas kernels: 19.2 us -> 18.1 us  [per_device(): pl.pallas_call(functools.partial(kernel, layers, bands, slots, half, cell...]
where the time goes in v1:
time: 20.5 us; the launch traced here: 20.3 us
  Pallas kernels  18.1 us (88%)
  local copies, waits for them, and re-layouts  1.48 us (7%)
  between operations  0.71 us (3%)
    pallas_call x1, Pallas kernels, per_device(): pl.pallas_call(functools.partial(kernel, layers, bands, slots, half, cell...  18.1 us
    unnamed x7, local copies, waits for them, and re-layouts  1.48 us

profile of v1, /device:TPU:0, one launch (start us, length us, event | category | flops | bytes accessed | tf_op | source)
XLA Modules:
  0.0 20.3 jit_solution(8812929032791859334)
XLA Ops:
  0.0 0.0 copy-start.2
  0.0 0.0 copy-start.1
  0.7 0.0 copy-done.2
  0.7 0.0 copy-done.1
  0.7 0.0 copy-start
  0.7 0.7 %copy-done = s32[4,6]{1,0:T(4,128)S(1)} copy-done((s32[4,6]{1,0:T(4,128)S(1)}, s32[4,6]{1,0:T(4,128)}, u32[]{:S(2)}) %copy-start) | copy-done | bytes 120
  1.4 18.1 %shard_map.64 = f32[1,4,32,1024]{3,2,1,0:T(8,128)S(1)} custom-call(s32[4,6]{1,0:T(4,128)S(1)} %copy-done, s32[1]{0:T(128)S(6)} %copy.8.counts_in, f32[2]{0:T(128)S(1)} %copy-done.1, f32[2]{0:T(128)S(1)} %copy-done.2, f32[1,4,32,1024]{3,2,1,0:T(8,128)} %ligand.1, s32[4,32,1024]{2,1,0:T(8,128)} %density.1), custom_call_target="tpu_custom_call" | custom-call | tf_op jit(solution)/shard_map/pallas_call | solution.py:412
  19.5 0.8 %copy.9 = f32[1,4,32,1024]{3,2,1,0:T(8,128)} copy(f32[1,4,32,1024]{3,2,1,0:T(8,128)S(1)} %shard_map.64) | data formatting | bytes 1048576
Async XLA Ops:
  0.0 0.7 %copy-start.2 = (f32[2]{0:T(128)S(1)}, f32[2]{0:T(128)}, u32[]{:S(2)}) copy-start(f32[2]{0:T(128)} %uptake_in.1) | copy-start | bytes 28
  0.0 0.7 %copy-start.1 = (f32[2]{0:T(128)S(1)}, f32[2]{0:T(128)}, u32[]{:S(2)}) copy-start(f32[2]{0:T(128)} %diffusion_in.1) | copy-start | bytes 28
  0.7 0.7 %copy-start = (s32[4,6]{1,0:T(4,128)S(1)}, s32[4,6]{1,0:T(4,128)}, u32[]{:S(2)}) copy-start(s32[4,6]{1,0:T(4,128)} %nbr_in.1) | copy-start | bytes 292

commit v2 on v1

--- a/solution.py
+++ b/solution.py
@@ -17,10 +17,13 @@
 def kernel(
     layers, bands, slots, half, cells,
     nbr_in, counts_in, diffusion_in, uptake_in, ligand, density, out,
-    field, dens, stage, y_high, y_low, y_minus, y_plus, z_low, z_high, z_minus, z_plus,
-    extra, y_first, y_here, z_first_low, z_first_high, nbr, counts, diffusion, uptake,
-    first_send, first_recv,
-    load_sem, small_sem, swap_send, swap_recv, face_send, face_recv, out_send, out_recv,
+    field, dens, y_low, y_high, y_minus, y_plus, z_low, z_high, z_minus, z_plus,
+    extra, y_first, y_here, z_first_low, z_first_high,
+    y_part, y_ghost, z_ghost_low, z_ghost_high,
+    y_last, y_last_here, y_last_minus, y_last_plus, z_last_minus, z_last_plus, z_near,
+    nbr, counts, diffusion, uptake,
+    first_send, first_recv, load_sem, small_sem, swap_send, swap_recv, face_send, face_recv,
+    last_send, last_recv, out_send, out_recv,
 ):
     core = lax.axis_index("pair")
     layer = lax.axis_index("cube")
@@ -79,7 +82,6 @@
             )
         )
         peers = peers + wanted.astype(jnp.int32)
-    pl.semaphore_wait(barrier, peers)
 
     swap = pltpu.make_async_remote_copy(
         src_ref=ligand.at[0, :, other_rows, :], dst_ref=field.at[0, core],
@@ -89,7 +91,6 @@
         src_ref=ligand.at[0, :, other_rows, :], dst_ref=field.at[0, other],
         send_sem=swap_send, recv_sem=swap_recv, device_id=partner_id, device_id_type=MESH,
     )
-    swap.start()
 
     def remote(source, target, step, k, device):
         return pltpu.make_async_remote_copy(
@@ -196,31 +197,18 @@
             total = piece if total is None else jnp.where(pair_of == m, piece, total)
         return total
 
-    def put_faces(step, tile, both):
-        packed = []
-        for species in range(2):
-            parts = both[species]
-            packed.append(pack(parts))
-            for j in range(columns):
-                at = slice(j * LANES, (j + 1) * LANES)
-                z_low[step, species, tile, :, at] = parts[j][:1]
-                z_high[step, species, tile, :, at] = parts[j][half - 1 :]
-        second = roll(packed[1], 1)
-        y_low[step, tile] = jnp.where(even, packed[0], second)
-        y_high[step, tile] = jnp.where(even, second, packed[0])
-
     def columns_of(value):
         return [value[:, j * LANES : (j + 1) * LANES] for j in range(columns)]
 
-    def first_faces(tile, carry):
-        for h, value in ((part, field[0, core, tile]), (rest, extra[tile])):
-            packed = pack(columns_of(value))
-            y_first[h, tile] = packed
-            z_first_low[h, tile] = value[:1]
-            z_first_high[h, tile] = value[half - 1 :]
-            if h is part:
-                y_here[core, tile] = packed
-        return carry
+    def first_faces():
+        for tile in range(slots):
+            for h, value in ((part, field[0, core, tile]), (rest, extra[tile])):
+                packed = pack(columns_of(value))
+                y_first[h, tile] = packed
+                z_first_low[h, tile : tile + 1, :] = value[:1]
+                z_first_high[h, tile : tile + 1, :] = value[half - 1 :]
+                if h is part:
+                    y_here[core, tile] = packed
 
     def other_faces(tile, carry):
         y_here[other, tile] = pack(columns_of(field[0, other, tile]))
@@ -243,7 +231,7 @@
         safe = jnp.maximum(value, 0)
         return value >= 0, lax.rem(safe, slots), safe // slots == block
 
-    def inner(step, tile):
+    def inner(step, tile, keep_faces):
         now, later = step % 2, (step + 1) % 2
         filled = tile < counts[0]
         left_ok, left, _ = entry(tile, 0)
@@ -269,6 +257,7 @@
             ghost_right = roll(field[now, species, right, :, :LANES], -EY)
             forward = [jnp.where(left_ok, ghost_left, zero)] + [roll(part, EY) for part in parts]
             backward = [roll(part, -EY) for part in parts] + [jnp.where(right_ok, ghost_right, zero)]
+            values = []
             for j in range(columns):
                 part = parts[j]
                 value = jnp.where(below_32, forward[j], forward[j + 1])
@@ -277,138 +266,270 @@
                 value = value + jnp.where(at_high, zero, roll(part, -1))
                 value = value + jnp.concatenate([blank, part[: half - 1]], axis=0)
                 value = value + jnp.concatenate([part[1:], blank], axis=0)
-                at = slice(j * LANES, (j + 1) * LANES)
-                field[later, species, tile, :, at] = (
-                    part * (keep - taken * share[j]) + rate * value
-                )
-
-    def outer(step, tile):
+                value = part * (keep - taken * share[j]) + rate * value
+                field[later, species, tile, :, j * LANES : (j + 1) * LANES] = value
+                values.append(value)
+            if keep_faces:
+                y_part[species, tile] = pack(values)
+
+    top = (half // ROWS - 1) * columns
+    sub = lax.broadcasted_iota(jnp.int32, (ROWS, LANES), 0)
+    in_low = jnp.logical_and(sub == 0, pair_of < columns)
+    in_high = jnp.logical_and(sub == ROWS - 1, pair_of >= top)
+    first_row = sub == 0
+    last_row = sub == ROWS - 1
+    row_pair = lax.rem(lax.broadcasted_iota(jnp.int32, (slots, LANES), 1) + 1, EY) // 2
+    row_edge = row_pair == 0
+
+    def pick(ok, ref, *at):
+        return jnp.where(ok, ref[at], zero)
+
+    def ghost_of(rate, from_front, from_back, shift):
+        return rate * jnp.where(
+            even, roll(from_front, 1 - EY - shift), roll(from_back, EY - 1 - shift)
+        )
+
+    def compact(step):
         later = (step + 1) % 2
-        filled = tile < counts[0]
-        front_ok, front, front_here = entry(tile, 2)
-        back_ok, back, back_here = entry(tile, 3)
-        lower_ok, lower, _ = entry(tile, 4)
-        upper_ok, upper, _ = entry(tile, 5)
         first = part == 0
-        lower = jnp.where(first, lower, tile)
-        lower_ok = jnp.where(first, lower_ok, filled)
-        upper = jnp.where(first, tile, upper)
-        upper_ok = jnp.where(first, filled, upper_ok)
-        result = []
+        for tile in range(slots):
+            filled = tile < counts[0]
+            front_ok, front, front_here = entry(tile, 2)
+            back_ok, back, back_here = entry(tile, 3)
+            lower_ok, lower, _ = entry(tile, 4)
+            upper_ok, upper, _ = entry(tile, 5)
+            lower = jnp.where(first, lower, tile)
+            lower_ok = jnp.where(first, lower_ok, filled)
+            upper = jnp.where(first, tile, upper)
+            upper_ok = jnp.where(first, filled, upper_ok)
+            for species in range(2):
+                rate = diffusion[species]
+                if step == 0:
+                    shift = 0
+                    from_front = jnp.where(
+                        front_here, y_here[species, front], y_minus[0][species, front])
+                    from_back = jnp.where(
+                        back_here, y_here[species, back], y_plus[0][species, back])
+                else:
+                    shift = species
+                    from_front = jnp.where(front_here, y_high[step, front], y_minus[step][front])
+                    from_back = jnp.where(back_here, y_low[step, back], y_plus[step][back])
+                from_front = jnp.where(front_ok, from_front, zero)
+                from_back = jnp.where(back_ok, from_back, zero)
+                y_ghost[species, tile] = ghost_of(rate, from_front, from_back, shift)
+                at = slice(tile, tile + 1)
+                below = rate * pick(lower_ok, z_minus[step], species, pl.ds(lower, 1), slice(None))
+                above = rate * pick(upper_ok, z_plus[step], species, pl.ds(upper, 1), slice(None))
+                z_ghost_low[species, at, :] = below
+                z_ghost_high[species, at, :] = above
+                z_low[step + 1, species, at, :] = field[later, species, tile, :1, :] + below
+                z_high[step + 1, species, at, :] = field[later, species, tile, half - 1 :, :] + above
+        packed = []
         for species in range(2):
-            rate = diffusion[species]
-            if step == 0:
-                shift = 0
-                from_front = jnp.where(front_here, y_here[species, front], y_minus[0][species, front])
-                from_back = jnp.where(back_here, y_here[species, back], y_plus[0][species, back])
-            else:
-                shift = species
-                from_front = jnp.where(front_here, y_high[step, front], y_minus[step][front])
-                from_back = jnp.where(back_here, y_low[step, back], y_plus[step][back])
-            from_front = jnp.where(front_ok, from_front, zero)
-            from_back = jnp.where(back_ok, from_back, zero)
-            ghost_y = rate * jnp.where(
-                even, roll(from_front, 1 - EY - shift), roll(from_back, EY - 1 - shift)
-            )
-            below = rate * jnp.where(lower_ok, z_minus[step][species, lower], zero)
-            above = rate * jnp.where(upper_ok, z_plus[step][species, upper], zero)
-            values = []
+            ghosts = [y_ghost[species, tile] for tile in range(slots)]
+            edge_low = jnp.concatenate([ghost[:1] for ghost in ghosts], axis=0)
+            edge_high = jnp.concatenate([ghost[ROWS - 1 :] for ghost in ghosts], axis=0)
+            pack_low = jnp.zeros((slots, LANES), jnp.float32)
+            pack_high = jnp.zeros((slots, LANES), jnp.float32)
             for j in range(columns):
                 at = slice(j * LANES, (j + 1) * LANES)
-                edge = jnp.concatenate(
-                    [roll(ghost_y, -2 * (zv * columns + j)) for zv in range(half // ROWS)], axis=0
-                )
-                value = field[later, species, tile, :, at] + jnp.where(at_edge, edge, zero)
-                value = value + jnp.where(row == 0, below[:, at], zero)
-                value = value + jnp.where(row == half - 1, above[:, at], zero)
-                values.append(value)
-            result.append(values)
-        return result
+                low = roll(z_ghost_low[species, :, at], 2 * j)
+                high = roll(z_ghost_high[species, :, at], 2 * (top + j))
+                pack_low = jnp.where(row_pair == j, low, pack_low)
+                pack_high = jnp.where(row_pair == top + j, high, pack_high)
+                z_low[step + 1, species, :, at] += jnp.where(row_edge, roll(edge_low, -2 * j), zero)
+                z_high[step + 1, species, :, at] += jnp.where(
+                    row_edge, roll(edge_high, -2 * (top + j)), zero)
+            packed.append([
+                y_part[species, tile] + ghosts[tile]
+                + jnp.where(in_low, jnp.broadcast_to(pack_low[tile : tile + 1], (ROWS, LANES)), zero)
+                + jnp.where(in_high, jnp.broadcast_to(pack_high[tile : tile + 1], (ROWS, LANES)), zero)
+                for tile in range(slots)
+            ])
+        for tile in range(slots):
+            if step + 1 == STEPS - 1:
+                for species in range(2):
+                    y_last[species, tile] = packed[species][tile]
+            else:
+                second = roll(packed[1][tile], 1)
+                y_low[step + 1, tile] = jnp.where(even, packed[0][tile], second)
+                y_high[step + 1, tile] = jnp.where(even, second, packed[0][tile])
 
     def inner_step(step):
         def body(tile, carry):
-            inner(step, tile)
+            inner(step, tile, step < STEPS - 1)
+            if step == STEPS - 1:
+                give(tile).start()
             return carry
 
         lax.fori_loop(0, slots, body, 0)
+
+    def completed(value, ghost, below, above, j):
+        pieces = []
+        for zv in range(half // ROWS):
+            piece = value[zv * ROWS : (zv + 1) * ROWS]
+            piece = piece + jnp.where(at_edge[:ROWS], roll(ghost, -2 * (zv * columns + j)), zero)
+            if zv == 0:
+                piece = piece + jnp.where(first_row, below, zero)
+            if zv == half // ROWS - 1:
+                piece = piece + jnp.where(last_row, above, zero)
+            pieces.append(piece)
+        return jnp.concatenate(pieces, axis=0)
 
     def outer_step(step):
         later = (step + 1) % 2
-
-        def body(tile, carry):
-            result = outer(step, tile)
+        for tile in range(slots):
             for species in range(2):
+                ghost = y_ghost[species, tile]
                 for j in range(columns):
                     at = slice(j * LANES, (j + 1) * LANES)
-                    field[later, species, tile, :, at] = result[species][j]
-            put_faces(step + 1, tile, result)
-            return carry
-
-        lax.fori_loop(0, slots, body, 0, unroll=True)
+                    field[later, species, tile, :, at] = completed(
+                        field[later, species, tile, :, at], ghost,
+                        z_ghost_low[species, tile : tile + 1, at],
+                        z_ghost_high[species, tile : tile + 1, at], j)
 
     def give(tile):
         return pltpu.make_async_remote_copy(
-            src_ref=stage.at[tile], dst_ref=out.at[0, tile, own_rows, :],
+            src_ref=field.at[STEPS % 2, other, tile], dst_ref=out.at[0, tile, own_rows, :],
             send_sem=out_send.at[tile], recv_sem=out_recv.at[tile],
             device_id=partner_id, device_id_type=MESH,
         )
 
     def take(tile):
         return pltpu.make_async_remote_copy(
-            src_ref=stage.at[tile], dst_ref=out.at[0, tile, other_rows, :],
+            src_ref=field.at[STEPS % 2, other, tile], dst_ref=out.at[0, tile, other_rows, :],
             send_sem=out_send.at[tile], recv_sem=out_recv.at[tile],
             device_id=partner_id, device_id_type=MESH,
         )
 
+    def last_copy(source, target, k, at, device):
+        return pltpu.make_async_remote_copy(
+            src_ref=source, dst_ref=target,
+            send_sem=last_send.at[k], recv_sem=last_recv.at[at],
+            device_id=device, device_id_type=MESH,
+        )
+
+    def last_sends():
+        end = STEPS - 1
+        both = jnp.logical_and
+        result = []
+        for s in range(2):
+            target = core * 0 + s
+            result += [
+                (both(part == 0, has_down), last_copy(
+                    z_low.at[end, s], z_last_plus, s, 0, {"cube": layer - 1, "pair": target})),
+                (both(part == 1, has_up), last_copy(
+                    z_high.at[end, s], z_last_minus, s, 1, {"cube": layer + 1, "pair": target})),
+                (has_plus, last_copy(
+                    y_last.at[s], y_last_minus.at[part], 2 + s, 2 + part,
+                    {"row": band + 1, "pair": target})),
+                (has_minus, last_copy(
+                    y_last.at[s], y_last_plus.at[part], 4 + s, 4 + part,
+                    {"row": band - 1, "pair": target})),
+            ]
+        return result + [
+            (always, last_copy(y_last.at[other], y_last_here, 6, 6, partner_id)),
+            (part == 0, last_copy(z_high.at[end, other], z_near, 7, 7, partner_id)),
+            (part == 1, last_copy(z_low.at[end, other], z_near, 7, 7, partner_id)),
+        ]
+
+    def last_receives():
+        arrivals = [(has_up, z_last_plus, 0), (has_down, z_last_minus, 1)]
+        for h in range(2):
+            arrivals.append((has_minus, y_last_minus.at[h], 2 + h))
+            arrivals.append((has_plus, y_last_plus.at[h], 4 + h))
+        arrivals += [(always, y_last_here, 6), (always, z_near, 7)]
+        return [(wanted, last_copy(ref, ref, 0, at, partner_id)) for wanted, ref, at in arrivals]
+
+    def last_step():
+        rate = diffusion[core]
+        first = part == 0
+        end = STEPS - 1
+        every = slice(None)
+        for tile in range(slots):
+            front_ok, front, front_here = entry(tile, 2)
+            back_ok, back, back_here = entry(tile, 3)
+            lower_ok, lower, _ = entry(tile, 4)
+            upper_ok, upper, _ = entry(tile, 5)
+            at = slice(tile, tile + 1)
+            bottom = pick(lower_ok, z_last_minus, pl.ds(lower, 1), every)
+            ceiling = pick(upper_ok, z_last_plus, pl.ds(upper, 1), every)
+            near = z_near[at, :]
+            mine = jnp.where(first, z_high[end, core, at, :], z_low[end, core, at, :])
+            for h, rows in ((part, own_rows), (rest, other_rows)):
+                if h is part:
+                    front_in, back_in = y_last[core, front], y_last[core, back]
+                    below = rate * jnp.where(first, bottom, near)
+                    above = rate * jnp.where(first, near, ceiling)
+                else:
+                    front_in, back_in = y_last_here[front], y_last_here[back]
+                    below = rate * jnp.where(first, mine, bottom)
+                    above = rate * jnp.where(first, ceiling, mine)
+                from_front = jnp.where(front_here, front_in, y_last_minus[h, front])
+                from_back = jnp.where(back_here, back_in, y_last_plus[h, back])
+                ghost = ghost_of(
+                    rate, jnp.where(front_ok, from_front, zero), jnp.where(back_ok, from_back, zero), 0)
+                for j in range(columns):
+                    lanes = slice(j * LANES, (j + 1) * LANES)
+                    if h is part:
+                        value = field[STEPS % 2, core, tile, :, lanes]
+                    else:
+                        value = out[0, tile, rows, lanes]
+                    out[0, tile, rows, lanes] = completed(
+                        value, ghost, below[:, lanes], above[:, lanes], j)
+
+    loads[0].wait()
+    loads[1].wait()
+    first_faces()
+    pl.semaphore_wait(barrier, peers)
+    for wanted, copy in first_sends():
+        pl.when(wanted)(copy.start)
+    swap.start()
+    own_planes()
     for load in smalls:
         load.wait()
-    loads[0].wait()
-    loads[1].wait()
-    lax.fori_loop(0, slots, first_faces, 0, unroll=True)
-    for wanted, copy in first_sends():
-        pl.when(wanted)(copy.start)
-    own_planes()
     loads[2].wait()
     swap_in.wait_recv()
     lax.fori_loop(0, slots, other_faces, 0, unroll=True)
-    for step in range(STEPS):
+    for step in range(STEPS - 1):
         inner_step(step)
         if step == 0:
             wait_first()
         else:
             wait_faces(step)
-        if step < STEPS - 1:
-            outer_step(step)
+        compact(step)
+        if step + 1 < STEPS - 1:
             send_faces(step + 1)
-
-    def last_body(tile, carry):
-        result = outer(STEPS - 1, tile)
-        for j in range(columns):
-            at = slice(j * LANES, (j + 1) * LANES)
-            stage[tile, :, at] = jnp.where(core == 0, result[1][j], result[0][j])
-        give(tile).start()
-        for j in range(columns):
-            at = slice(j * LANES, (j + 1) * LANES)
-            out[0, tile, own_rows, at] = jnp.where(core == 0, result[0][j], result[1][j])
-        return carry
-
-    lax.fori_loop(0, slots, last_body, 0, unroll=True)
+        else:
+            for wanted, copy in last_sends():
+                pl.when(wanted)(copy.start)
+        outer_step(step)
+    inner_step(STEPS - 1)
+    for tile in range(slots):
+        take(tile).wait_recv()
+    for wanted, copy in last_receives():
+        pl.when(wanted)(copy.wait_recv)
+    last_step()
     swap.wait_send()
     for wanted, copy in first_sends():
         pl.when(wanted)(copy.wait_send)
-    for step in range(1, STEPS):
+    for step in range(1, STEPS - 1):
         wait_sent(step)
+    for wanted, copy in last_sends():
+        pl.when(wanted)(copy.wait_send)
     for tile in range(slots):
         give(tile).wait_send()
-        take(tile).wait_recv()
 
 
 def per_device(layers, bands, ligand, density, counts, neighbours, diffusion, uptake):
     _, slots, depth, cells = ligand.shape
     half = depth // 2
     faces = (slots, ROWS, LANES)
-    planes = (2, slots, 1, cells)
+    planes = (2, slots, cells)
     away = pl.BlockSpec(memory_space=pltpu.HBM)
+    neighbours, diffusion, uptake = [
+        pltpu.with_memory_space_constraint(x, pltpu.HBM) for x in (neighbours, diffusion, uptake)
+    ]
     return pl.pallas_call(
         functools.partial(kernel, layers, bands, slots, half, cells),
         out_shape=jax.ShapeDtypeStruct(ligand.shape, jnp.float32),
@@ -417,20 +538,30 @@
         scratch_shapes=[
             pltpu.VMEM((2, 2, slots, half, cells), jnp.float32),
             pltpu.VMEM((slots, half, cells), jnp.int32),
-            pltpu.VMEM((slots, half, cells), jnp.float32),
             pltpu.VMEM((STEPS,) + faces, jnp.float32),
             pltpu.VMEM((STEPS,) + faces, jnp.float32),
-            [pltpu.VMEM((2,) + faces, jnp.float32)] + [pltpu.VMEM(faces, jnp.float32)] * (STEPS - 1),
-            [pltpu.VMEM((2,) + faces, jnp.float32)] + [pltpu.VMEM(faces, jnp.float32)] * (STEPS - 1),
+            [pltpu.VMEM((2,) + faces, jnp.float32)] + [pltpu.VMEM(faces, jnp.float32)] * (STEPS - 2),
+            [pltpu.VMEM((2,) + faces, jnp.float32)] + [pltpu.VMEM(faces, jnp.float32)] * (STEPS - 2),
             pltpu.VMEM((STEPS,) + planes, jnp.float32),
             pltpu.VMEM((STEPS,) + planes, jnp.float32),
-            [pltpu.VMEM(planes, jnp.float32)] * STEPS,
-            [pltpu.VMEM(planes, jnp.float32)] * STEPS,
+            [pltpu.VMEM(planes, jnp.float32)] * (STEPS - 1),
+            [pltpu.VMEM(planes, jnp.float32)] * (STEPS - 1),
             pltpu.VMEM((slots, half, cells), jnp.float32),
             pltpu.VMEM((2,) + faces, jnp.float32),
             pltpu.VMEM((2,) + faces, jnp.float32),
             pltpu.VMEM(planes, jnp.float32),
             pltpu.VMEM(planes, jnp.float32),
+            pltpu.VMEM((2,) + faces, jnp.float32),
+            pltpu.VMEM((2,) + faces, jnp.float32),
+            pltpu.VMEM(planes, jnp.float32),
+            pltpu.VMEM(planes, jnp.float32),
+            pltpu.VMEM((2,) + faces, jnp.float32),
+            pltpu.VMEM(faces, jnp.float32),
+            pltpu.VMEM((2,) + faces, jnp.float32),
+            pltpu.VMEM((2,) + faces, jnp.float32),
+            pltpu.VMEM((slots, cells), jnp.float32),
+            pltpu.VMEM((slots, cells), jnp.float32),
+            pltpu.VMEM((slots, cells), jnp.float32),
             pltpu.SMEM((slots, 6), jnp.int32),
             pltpu.SMEM((1,), jnp.int32),
             pltpu.SMEM((2,), jnp.float32),
@@ -443,6 +574,8 @@
             pltpu.SemaphoreType.DMA,
             pltpu.SemaphoreType.DMA((STEPS, 4)),
             pltpu.SemaphoreType.DMA((STEPS, 4)),
+            pltpu.SemaphoreType.DMA((8,)),
+            pltpu.SemaphoreType.DMA((8,)),
             pltpu.SemaphoreType.DMA((slots,)),
             pltpu.SemaphoreType.DMA((slots,)),
         ],

time: 20.5 us -> 18 us (0.88)
  Pallas kernels: 18.1 us -> 16.4 us
  local copies, waits for them, and re-layouts: 1.48 us -> 0.8 us
    pallas_call x1, Pallas kernels: 18.1 us -> 16.4 us  [per_device(): pl.pallas_call(functools.partial(kernel, layers, bands, slots, half, cell...]
    unnamed x7 -> x1, local copies, waits for them, and re-layouts: 1.48 us -> 0.8 us
where the time goes in v2:
time: 18 us; the launch traced here: 17.8 us
  Pallas kernels  16.4 us (91%)
  local copies, waits for them, and re-layouts  0.8 us (4%)
  between operations  0.66 us (4%)
    pallas_call x1, Pallas kernels, per_device(): pl.pallas_call(functools.partial(kernel, layers, bands, slots, half, cell...  16.4 us
    unnamed x1, local copies, waits for them, and re-layouts  0.8 us

profile of v2, /device:TPU:0, one launch (start us, length us, event | category | flops | bytes accessed | tf_op | source)
XLA Modules:
  0.0 17.8 jit_solution(9481493867081970572)
XLA Ops:
  0.7 16.4 %shard_map.64 = f32[1,4,32,1024]{3,2,1,0:T(8,128)S(1)} custom-call(s32[4,6]{1,0:T(4,128)} %nbr_in.1, s32[1]{0:T(128)S(6)} %copy.8.counts_in, f32[2]{0:T(128)} %diffusion_in.1, f32[2]{0:T(128)} %uptake_in.1, f32[1,4,32,1024]{3,2,1,0:T(8,128)} %ligand.1, s32[4,32,1024]{2,1,0:T(8,128)} %density.1), custom_call_target="tpu_custom_call" | custom-call | tf_op jit(solution)/shard_map/pallas_call | solution.py:533
  17.0 0.8 %copy.9 = f32[1,4,32,1024]{3,2,1,0:T(8,128)} copy(f32[1,4,32,1024]{3,2,1,0:T(8,128)S(1)} %shard_map.64) | data formatting | bytes 1048576

commit v3 on v2

--- a/solution.py
+++ b/solution.py
@@ -9,6 +9,7 @@
 
 EY = 32
 STEPS = 4
+DONE = {1: 1, 2: 4, 3: 3}
 LANES = 128
 ROWS = 8
 MESH = pl.DeviceIdType.MESH
@@ -21,9 +22,11 @@
     extra, y_first, y_here, z_first_low, z_first_high,
     y_part, y_ghost, z_ghost_low, z_ghost_high,
     y_last, y_last_here, y_last_minus, y_last_plus, z_last_minus, z_last_plus, z_near,
+    line_high, line_low, solved_high, solved_low, near_front, near_back, far_front, far_back,
+    g_front, g_back, g_below, g_above, weights,
     nbr, counts, diffusion, uptake,
     first_send, first_recv, load_sem, small_sem, swap_send, swap_recv, face_send, face_recv,
-    last_send, last_recv, out_send, out_recv,
+    line_send, line_recv, last_send, last_recv, out_send, out_recv,
 ):
     core = lax.axis_index("pair")
     layer = lax.axis_index("cube")
@@ -73,6 +76,8 @@
         (has_plus, plus_id),
         (has_minus, {"row": band - 1}),
         (has_plus, {"row": band + 1}),
+        (jnp.logical_and(has_minus, has_far), {"row": band - 1, "cube": far_layer}),
+        (jnp.logical_and(has_plus, has_far), {"row": band + 1, "cube": far_layer}),
     ]
     peers = jnp.int32(0)
     for wanted, device in greeted:
@@ -231,17 +236,53 @@
         safe = jnp.maximum(value, 0)
         return value >= 0, lax.rem(safe, slots), safe // slots == block
 
+    def make_weights():
+        source = lax.broadcasted_iota(jnp.int32, (2 * LANES, 2 * LANES), 0)
+        target = lax.broadcasted_iota(jnp.int32, (2 * LANES, 2 * LANES), 1)
+        apart = jnp.abs(source - target)
+        same = source // EY == target // EY
+        near = jnp.logical_or(apart == EY, jnp.logical_and(apart == 1, same))
+        inside = jnp.where(near, 1.0, 0.0).astype(jnp.bfloat16)
+        source = lax.broadcasted_iota(jnp.int32, (LANES, 2 * LANES), 0)
+        target = lax.broadcasted_iota(jnp.int32, (LANES, 2 * LANES), 1)
+        after = jnp.logical_and(source < EY, target == source + 2 * LANES - EY)
+        before = jnp.logical_and(source >= LANES - EY, target == source - LANES + EY)
+        beside = jnp.where(jnp.logical_or(after, before), 1.0, 0.0).astype(jnp.bfloat16)
+        weights[: 2 * LANES, :] = inside
+        weights[2 * LANES : 4 * LANES, :] = inside
+        weights[4 * LANES : 5 * LANES, :] = beside
+        weights[5 * LANES :, :] = beside
+
+    def halves(value):
+        high = value.astype(jnp.bfloat16)
+        return high, (value - high.astype(jnp.float32)).astype(jnp.bfloat16)
+
+    blocks = columns // 2
+
     def inner(step, tile, keep_faces):
         now, later = step % 2, (step + 1) % 2
         filled = tile < counts[0]
         left_ok, left, _ = entry(tile, 0)
         right_ok, right, _ = entry(tile, 1)
-        fields = []
+        fields, lefts = [], []
         for species in range(2):
             parts = columns_of(field[now, species, tile])
             if step == 0:
                 parts = [jnp.where(filled, part, zero) for part in parts]
             fields.append(parts)
+            ends = [
+                jnp.where(left_ok, field[now, species, left, :, cells - LANES :], zero)
+            ] + parts + [
+                jnp.where(right_ok, field[now, species, right, :, :LANES], zero)
+            ]
+            split = [halves(part) for part in parts]
+            for b in range(blocks):
+                beside = halves(jnp.where(below_32, ends[2 * b + 3], ends[2 * b]))
+                lefts.append(jnp.concatenate([
+                    split[2 * b][0], split[2 * b + 1][0], split[2 * b][1], split[2 * b + 1][1],
+                    beside[0], beside[1]], axis=1))
+        sums = jnp.dot(
+            jnp.concatenate(lefts, axis=0), weights[...], preferred_element_type=jnp.float32)
         amount = columns_of(dens[tile])
         share = [
             amount[j].astype(jnp.float32) / (1.0 + fields[0][j] + fields[1][j])
@@ -253,17 +294,11 @@
             rate = diffusion[species]
             keep = 1.0 - 6.0 * rate
             taken = uptake[species] * 0.125
-            ghost_left = roll(field[now, species, left, :, cells - LANES :], EY)
-            ghost_right = roll(field[now, species, right, :, :LANES], -EY)
-            forward = [jnp.where(left_ok, ghost_left, zero)] + [roll(part, EY) for part in parts]
-            backward = [roll(part, -EY) for part in parts] + [jnp.where(right_ok, ghost_right, zero)]
             values = []
             for j in range(columns):
                 part = parts[j]
-                value = jnp.where(below_32, forward[j], forward[j + 1])
-                value = value + jnp.where(above_96, backward[j + 1], backward[j])
-                value = value + jnp.where(at_low, zero, roll(part, 1))
-                value = value + jnp.where(at_high, zero, roll(part, -1))
+                at = (species * blocks + j // 2) * half
+                value = sums[at : at + half, (j % 2) * LANES : (j % 2 + 1) * LANES]
                 value = value + jnp.concatenate([blank, part[: half - 1]], axis=0)
                 value = value + jnp.concatenate([part[1:], blank], axis=0)
                 value = part * (keep - taken * share[j]) + rate * value
@@ -290,6 +325,7 @@
         )
 
     def compact(step):
+        into = DONE[step + 1]
         later = (step + 1) % 2
         first = part == 0
         for tile in range(slots):
@@ -310,20 +346,30 @@
                         front_here, y_here[species, front], y_minus[0][species, front])
                     from_back = jnp.where(
                         back_here, y_here[species, back], y_plus[0][species, back])
-                else:
+                elif step == 1:
                     shift = species
                     from_front = jnp.where(front_here, y_high[step, front], y_minus[step][front])
                     from_back = jnp.where(back_here, y_low[step, back], y_plus[step][back])
+                else:
+                    shift = species
+                    from_front = jnp.where(front_here, y_high[DONE[step], front], g_front[tile])
+                    from_back = jnp.where(back_here, y_low[DONE[step], back], g_back[tile])
                 from_front = jnp.where(front_ok, from_front, zero)
                 from_back = jnp.where(back_ok, from_back, zero)
                 y_ghost[species, tile] = ghost_of(rate, from_front, from_back, shift)
                 at = slice(tile, tile + 1)
-                below = rate * pick(lower_ok, z_minus[step], species, pl.ds(lower, 1), slice(None))
-                above = rate * pick(upper_ok, z_plus[step], species, pl.ds(upper, 1), slice(None))
+                if step < 2:
+                    below = pick(lower_ok, z_minus[step], species, pl.ds(lower, 1), slice(None))
+                    above = pick(upper_ok, z_plus[step], species, pl.ds(upper, 1), slice(None))
+                else:
+                    below = pick(lower_ok, g_below, species, at, slice(None))
+                    above = pick(upper_ok, g_above, species, at, slice(None))
+                below = rate * below
+                above = rate * above
                 z_ghost_low[species, at, :] = below
                 z_ghost_high[species, at, :] = above
-                z_low[step + 1, species, at, :] = field[later, species, tile, :1, :] + below
-                z_high[step + 1, species, at, :] = field[later, species, tile, half - 1 :, :] + above
+                z_low[into, species, at, :] = field[later, species, tile, :1, :] + below
+                z_high[into, species, at, :] = field[later, species, tile, half - 1 :, :] + above
         packed = []
         for species in range(2):
             ghosts = [y_ghost[species, tile] for tile in range(slots)]
@@ -337,8 +383,8 @@
                 high = roll(z_ghost_high[species, :, at], 2 * (top + j))
                 pack_low = jnp.where(row_pair == j, low, pack_low)
                 pack_high = jnp.where(row_pair == top + j, high, pack_high)
-                z_low[step + 1, species, :, at] += jnp.where(row_edge, roll(edge_low, -2 * j), zero)
-                z_high[step + 1, species, :, at] += jnp.where(
+                z_low[into, species, :, at] += jnp.where(row_edge, roll(edge_low, -2 * j), zero)
+                z_high[into, species, :, at] += jnp.where(
                     row_edge, roll(edge_high, -2 * (top + j)), zero)
             packed.append([
                 y_part[species, tile] + ghosts[tile]
@@ -352,17 +398,164 @@
                     y_last[species, tile] = packed[species][tile]
             else:
                 second = roll(packed[1][tile], 1)
-                y_low[step + 1, tile] = jnp.where(even, packed[0][tile], second)
-                y_high[step + 1, tile] = jnp.where(even, second, packed[0][tile])
+                y_low[into, tile] = jnp.where(even, packed[0][tile], second)
+                y_high[into, tile] = jnp.where(even, second, packed[0][tile])
+
+    lines = lax.broadcasted_iota(jnp.int32, (slots, LANES), 1)
+    line_even = lax.rem(lines, 2) == 0
+    in_low_format = lax.rem(lane, EY) // 2
+
+    def rows_of(rows):
+        return jnp.concatenate(rows, axis=0)
+
+    def line_ghost(rate, from_front, from_back, shift):
+        return rate * jnp.where(
+            line_even, roll(from_front, 1 - EY - shift), roll(from_back, EY - 1 - shift)
+        )
+
+    def line_copy(source, target, k, device):
+        return pltpu.make_async_remote_copy(
+            src_ref=source, dst_ref=target, send_sem=line_send.at[k], recv_sem=line_recv.at[k],
+            device_id=device, device_id_type=MESH,
+        )
+
+    def line_messages():
+        both = jnp.logical_and
+        out_and_in = [
+            (has_plus, has_minus, line_high, near_front, {"row": band + 1}),
+            (has_minus, has_plus, line_low, near_back, {"row": band - 1}),
+            (both(has_plus, has_far), both(has_minus, has_far), solved_high, far_front,
+             {"row": band + 1, "cube": far_layer}),
+            (both(has_minus, has_far), both(has_plus, has_far), solved_low, far_back,
+             {"row": band - 1, "cube": far_layer}),
+        ]
+        return [
+            (sent, received, line_copy(source, target, k, device))
+            for k, (sent, received, source, target, device) in enumerate(out_and_in)
+        ]
+
+    def make_lines():
+        for tile in range(slots):
+            at = slice(tile, tile + 1)
+            high, low = y_high[1, tile], y_low[1, tile]
+            line_high[at, :] = jnp.where(pair_of[:1] < columns, high[:1], high[ROWS - 1 :])
+            line_low[at, :] = jnp.where(in_low_format[:1] < columns, low[:1], low[ROWS - 1 :])
+        for k, column in ((0, None), (1, 3)):
+            solve(line_high, solved_high, k, column)
+        for k, column in ((0, None), (1, 2)):
+            solve(line_low, solved_low, k, column)
+
+    def solve(line, solved, k, column):
+        names = []
+        for tile in range(slots):
+            if column is None:
+                value = jnp.where(part == 0, nbr[tile, 4], nbr[tile, 5])
+                names.append(jnp.where(value >= 0, lax.rem(jnp.maximum(value, 0), slots), -1))
+            else:
+                ok, slot, here = entry(tile, column)
+                names.append(jnp.where(jnp.logical_and(ok, jnp.logical_not(here)), slot, -1))
+        found = lax.broadcasted_iota(jnp.int32, (slots, LANES), 0)
+        total = jnp.zeros((slots, LANES), jnp.float32)
+        for tile in range(slots):
+            row = jnp.broadcast_to(line[tile : tile + 1, :], (slots, LANES))
+            total = total + jnp.where(found == names[tile], row, zero)
+        solved[k] = total
+
+    def partial_faces(step):
+        later = (step + 1) % 2
+        into = step + 1
+        fronts, backs = [], []
+        for tile in range(slots):
+            second = roll(y_part[1, tile], 1)
+            y_low[into, tile] = jnp.where(even, y_part[0, tile], second)
+            y_high[into, tile] = jnp.where(even, second, y_part[0, tile])
+            front_ok, front, front_here = entry(tile, 2)
+            back_ok, back, back_here = entry(tile, 3)
+            both = jnp.logical_and
+            fronts.append(pick(both(front_ok, front_here), line_high, pl.ds(front, 1), slice(None)))
+            backs.append(pick(both(back_ok, back_here), line_low, pl.ds(back, 1), slice(None)))
+            for species in range(2):
+                at = slice(tile, tile + 1)
+                z_low[into, species, at, :] = field[later, species, tile, :1, :]
+                z_high[into, species, at, :] = field[later, species, tile, half - 1 :, :]
+        fronts, backs = rows_of(fronts), rows_of(backs)
+        for species in range(2):
+            edge = line_ghost(diffusion[species], fronts, backs, species)
+            for j in range(columns):
+                at = slice(j * LANES, (j + 1) * LANES)
+                z_low[into, species, :, at] += jnp.where(row_edge, roll(edge, -2 * j), zero)
+                z_high[into, species, :, at] += jnp.where(
+                    row_edge, roll(edge, -2 * (top + j)), zero)
+
+    def complete(step):
+        first = part == 0
+        both = jnp.logical_and
+        every = slice(None)
+        shift = 2 * top
+        low_even_rate = jnp.where(even, diffusion[0], diffusion[1])
+        high_even_rate = jnp.where(even, diffusion[1], diffusion[0])
+        below_front, below_back, above_front, above_back = [], [], [], []
+        for tile in range(slots):
+            front_ok, front, front_here = entry(tile, 2)
+            back_ok, back, back_here = entry(tile, 3)
+            lower_ok, lower, _ = entry(tile, 4)
+            upper_ok, upper, _ = entry(tile, 5)
+            far = jnp.where(first, lower, upper)
+            far_ok = jnp.where(first, lower_ok, upper_ok)
+            front_cross = both(front_ok, jnp.logical_not(front_here))
+            back_cross = both(back_ok, jnp.logical_not(back_here))
+            near_f = pick(front_cross, near_front, pl.ds(front, 1), every)
+            near_b = pick(back_cross, near_back, pl.ds(back, 1), every)
+            side_f = pick(both(front_cross, has_far), far_front, 0, pl.ds(front, 1), every)
+            side_b = pick(both(back_cross, has_far), far_back, 0, pl.ds(back, 1), every)
+            far_f = pick(both(far_ok, has_minus), far_front, 1, pl.ds(far, 1), every)
+            far_b = pick(both(far_ok, has_plus), far_back, 1, pl.ds(far, 1), every)
+            below_front.append(jnp.where(first, far_f, near_f))
+            above_front.append(jnp.where(first, near_f, far_f))
+            below_back.append(jnp.where(first, far_b, near_b))
+            above_back.append(jnp.where(first, near_b, far_b))
+
+            def placed(near, side, form):
+                low = roll(jnp.broadcast_to(jnp.where(first, side, near), (ROWS, LANES)), -shift)
+                high = roll(jnp.broadcast_to(jnp.where(first, near, side), (ROWS, LANES)), shift)
+                low = jnp.where(both(sub == 0, form < columns), low, zero)
+                return low + jnp.where(both(sub == ROWS - 1, form >= top), high, zero)
+
+            g_front[tile] = jnp.where(
+                front_cross,
+                y_minus[step + 1][front] + high_even_rate * (
+                    roll(y_low[step, tile], EY - 1) + placed(near_f, side_f, pair_of)),
+                zero)
+            g_back[tile] = jnp.where(
+                back_cross,
+                y_plus[step + 1][back] + low_even_rate * (
+                    roll(y_high[step, tile], 1 - EY) + placed(near_b, side_b, in_low_format)),
+                zero)
+            lower = jnp.where(first, lower, tile)
+            upper = jnp.where(first, tile, upper)
+            for species in range(2):
+                rate = diffusion[species]
+                at = slice(tile, tile + 1)
+                g_below[species, at, :] = (
+                    z_minus[step + 1][species, pl.ds(lower, 1), :] + rate * z_low[step, species, at, :])
+                g_above[species, at, :] = (
+                    z_plus[step + 1][species, pl.ds(upper, 1), :] + rate * z_high[step, species, at, :])
+        below_front, below_back = rows_of(below_front), rows_of(below_back)
+        above_front, above_back = rows_of(above_front), rows_of(above_back)
+        for species in range(2):
+            below = line_ghost(diffusion[species], below_front, below_back, species)
+            above = line_ghost(diffusion[species], above_front, above_back, species)
+            for j in range(columns):
+                at = slice(j * LANES, (j + 1) * LANES)
+                g_below[species, :, at] += jnp.where(
+                    row_edge, roll(below, -2 * (top + j)), zero)
+                g_above[species, :, at] += jnp.where(row_edge, roll(above, -2 * j), zero)
 
     def inner_step(step):
-        def body(tile, carry):
+        for tile in range(slots):
             inner(step, tile, step < STEPS - 1)
             if step == STEPS - 1:
                 give(tile).start()
-            return carry
-
-        lax.fori_loop(0, slots, body, 0)
 
     def completed(value, ghost, below, above, j):
         pieces = []
@@ -480,6 +673,7 @@
 
     loads[0].wait()
     loads[1].wait()
+    make_weights()
     first_faces()
     pl.semaphore_wait(barrier, peers)
     for wanted, copy in first_sends():
@@ -491,19 +685,29 @@
     loads[2].wait()
     swap_in.wait_recv()
     lax.fori_loop(0, slots, other_faces, 0, unroll=True)
-    for step in range(STEPS - 1):
-        inner_step(step)
-        if step == 0:
-            wait_first()
-        else:
-            wait_faces(step)
-        compact(step)
-        if step + 1 < STEPS - 1:
-            send_faces(step + 1)
-        else:
-            for wanted, copy in last_sends():
-                pl.when(wanted)(copy.start)
-        outer_step(step)
+    inner_step(0)
+    wait_first()
+    compact(0)
+    send_faces(1)
+    make_lines()
+    for sent, _, copy in line_messages():
+        pl.when(sent)(copy.start)
+    outer_step(0)
+    inner_step(1)
+    partial_faces(1)
+    send_faces(2)
+    wait_faces(1)
+    compact(1)
+    outer_step(1)
+    inner_step(2)
+    wait_faces(2)
+    for _, received, copy in line_messages():
+        pl.when(received)(copy.wait_recv)
+    complete(1)
+    compact(2)
+    for wanted, copy in last_sends():
+        pl.when(wanted)(copy.start)
+    outer_step(2)
     inner_step(STEPS - 1)
     for tile in range(slots):
         take(tile).wait_recv()
@@ -515,6 +719,8 @@
         pl.when(wanted)(copy.wait_send)
     for step in range(1, STEPS - 1):
         wait_sent(step)
+    for sent, _, copy in line_messages():
+        pl.when(sent)(copy.wait_send)
     for wanted, copy in last_sends():
         pl.when(wanted)(copy.wait_send)
     for tile in range(slots):
@@ -538,12 +744,12 @@
         scratch_shapes=[
             pltpu.VMEM((2, 2, slots, half, cells), jnp.float32),
             pltpu.VMEM((slots, half, cells), jnp.int32),
-            pltpu.VMEM((STEPS,) + faces, jnp.float32),
-            pltpu.VMEM((STEPS,) + faces, jnp.float32),
+            pltpu.VMEM((STEPS + 1,) + faces, jnp.float32),
+            pltpu.VMEM((STEPS + 1,) + faces, jnp.float32),
             [pltpu.VMEM((2,) + faces, jnp.float32)] + [pltpu.VMEM(faces, jnp.float32)] * (STEPS - 2),
             [pltpu.VMEM((2,) + faces, jnp.float32)] + [pltpu.VMEM(faces, jnp.float32)] * (STEPS - 2),
-            pltpu.VMEM((STEPS,) + planes, jnp.float32),
-            pltpu.VMEM((STEPS,) + planes, jnp.float32),
+            pltpu.VMEM((STEPS + 1,) + planes, jnp.float32),
+            pltpu.VMEM((STEPS + 1,) + planes, jnp.float32),
             [pltpu.VMEM(planes, jnp.float32)] * (STEPS - 1),
             [pltpu.VMEM(planes, jnp.float32)] * (STEPS - 1),
             pltpu.VMEM((slots, half, cells), jnp.float32),
@@ -562,6 +768,19 @@
             pltpu.VMEM((slots, cells), jnp.float32),
             pltpu.VMEM((slots, cells), jnp.float32),
             pltpu.VMEM((slots, cells), jnp.float32),
+            pltpu.VMEM((slots, LANES), jnp.float32),
+            pltpu.VMEM((slots, LANES), jnp.float32),
+            pltpu.VMEM((2, slots, LANES), jnp.float32),
+            pltpu.VMEM((2, slots, LANES), jnp.float32),
+            pltpu.VMEM((slots, LANES), jnp.float32),
+            pltpu.VMEM((slots, LANES), jnp.float32),
+            pltpu.VMEM((2, slots, LANES), jnp.float32),
+            pltpu.VMEM((2, slots, LANES), jnp.float32),
+            pltpu.VMEM(faces, jnp.float32),
+            pltpu.VMEM(faces, jnp.float32),
+            pltpu.VMEM(planes, jnp.float32),
+            pltpu.VMEM(planes, jnp.float32),
+            pltpu.VMEM((6 * LANES, 2 * LANES), jnp.bfloat16),
             pltpu.SMEM((slots, 6), jnp.int32),
             pltpu.SMEM((1,), jnp.int32),
             pltpu.SMEM((2,), jnp.float32),
@@ -574,6 +793,8 @@
             pltpu.SemaphoreType.DMA,
             pltpu.SemaphoreType.DMA((STEPS, 4)),
             pltpu.SemaphoreType.DMA((STEPS, 4)),
+            pltpu.SemaphoreType.DMA((4,)),
+            pltpu.SemaphoreType.DMA((4,)),
             pltpu.SemaphoreType.DMA((8,)),
             pltpu.SemaphoreType.DMA((8,)),
             pltpu.SemaphoreType.DMA((slots,)),

time: 18 us -> 16.5 us (0.917)
  Pallas kernels: 16.4 us -> 14.9 us
    pallas_call x1, Pallas kernels: 16.4 us -> 14.9 us  [per_device(): pl.pallas_call(functools.partial(kernel, layers, bands, slots, half, cell...]
where the time goes in v3:
time: 16.5 us; the launch traced here: 16.3 us
  Pallas kernels  14.9 us (90%)
  local copies, waits for them, and re-layouts  0.8 us (5%)
  between operations  0.66 us (4%)
    pallas_call x1, Pallas kernels, per_device(): pl.pallas_call(functools.partial(kernel, layers, bands, slots, half, cell...  14.9 us
    unnamed x1, local copies, waits for them, and re-layouts  0.8 us

profile of v3, /device:TPU:0, one launch (start us, length us, event | category | flops | bytes accessed | tf_op | source)
XLA Modules:
  0.0 16.3 jit_solution(15648810076392211272)
XLA Ops:
  0.7 14.9 %shard_map.64 = f32[1,4,32,1024]{3,2,1,0:T(8,128)S(1)} custom-call(s32[4,6]{1,0:T(4,128)} %nbr_in.1, s32[1]{0:T(128)S(6)} %copy.8.counts_in, f32[2]{0:T(128)} %diffusion_in.1, f32[2]{0:T(128)} %uptake_in.1, f32[1,4,32,1024]{3,2,1,0:T(8,128)} %ligand.1, s32[4,32,1024]{2,1,0:T(8,128)} %density.1), custom_call_target="tpu_custom_call" | custom-call | tf_op jit(solution)/shard_map/pallas_call | solution.py:739
  15.5 0.8 %copy.9 = f32[1,4,32,1024]{3,2,1,0:T(8,128)} copy(f32[1,4,32,1024]{3,2,1,0:T(8,128)S(1)} %shard_map.64) | data formatting | bytes 1048576

commit v4 on v3

--- a/solution.py
+++ b/solution.py
@@ -19,9 +19,9 @@
     layers, bands, slots, half, cells,
     nbr_in, counts_in, diffusion_in, uptake_in, ligand, density, out,
     field, dens, y_low, y_high, y_minus, y_plus, z_low, z_high, z_minus, z_plus,
-    extra, y_first, y_here, z_first_low, z_first_high,
+    extra, y_first_low, y_first_high, y_here, z_first_low, z_first_high,
     y_part, y_ghost, z_ghost_low, z_ghost_high,
-    y_last, y_last_here, y_last_minus, y_last_plus, z_last_minus, z_last_plus, z_near,
+    y_last, y_last_low, y_last_high, y_last_here, y_last_minus, y_last_plus, z_last_minus, z_last_plus, z_near,
     line_high, line_low, solved_high, solved_low, near_front, near_back, far_front, far_back,
     g_front, g_back, g_below, g_above, weights,
     nbr, counts, diffusion, uptake,
@@ -60,8 +60,6 @@
             [(nbr_in, nbr), (counts_in, counts), (diffusion_in, diffusion), (uptake_in, uptake)]
         )
     ]
-    for load in loads + smalls:
-        load.start()
 
     barrier = pltpu.get_barrier_semaphore()
     has_down = layer > 0
@@ -88,6 +86,9 @@
         )
         peers = peers + wanted.astype(jnp.int32)
 
+    for load in loads + smalls:
+        load.start()
+
     swap = pltpu.make_async_remote_copy(
         src_ref=ligand.at[0, :, other_rows, :], dst_ref=field.at[0, core],
         send_sem=swap_send, recv_sem=swap_recv, device_id=partner_id, device_id_type=MESH,
@@ -133,20 +134,20 @@
 
     def first_sends():
         return [
-            (part == 0, first_copy(z_first_high.at[0], z_minus[0], 0, 0, partner_id)),
-            (part == 1, first_copy(z_first_low.at[1], z_plus[0], 1, 1, partner_id)),
+            (has_plus, first_copy(
+                y_first_high.at[h], y_minus[0], 4 + h, 2, {"row": band + 1, "pair": lax.rem(band + 1 + h, 2)}))
+            for h in range(2)
+        ] + [
+            (has_minus, first_copy(
+                y_first_low.at[h], y_plus[0], 6 + h, 3, {"row": band - 1, "pair": lax.rem(band + 1 + h, 2)}))
+            for h in range(2)
+        ] + [
             (has_down, first_copy(
                 z_first_low.at[0], z_plus[0], 2, 1, {"cube": layer - 1, "pair": high_core})),
             (has_up, first_copy(
                 z_first_high.at[1], z_minus[0], 3, 0, {"cube": layer + 1, "pair": low_core})),
-        ] + [
-            (has_plus, first_copy(
-                y_first.at[h], y_minus[0], 4 + h, 2, {"row": band + 1, "pair": lax.rem(band + 1 + h, 2)}))
-            for h in range(2)
-        ] + [
-            (has_minus, first_copy(
-                y_first.at[h], y_plus[0], 6 + h, 3, {"row": band - 1, "pair": lax.rem(band + 1 + h, 2)}))
-            for h in range(2)
+            (part == 0, first_copy(z_first_high.at[0], z_minus[0], 0, 0, partner_id)),
+            (part == 1, first_copy(z_first_low.at[1], z_plus[0], 1, 1, partner_id)),
         ]
 
     def arrived(target, at, species):
@@ -205,15 +206,23 @@
     def columns_of(value):
         return [value[:, j * LANES : (j + 1) * LANES] for j in range(columns)]
 
+    def in_pairs(packed, low, high):
+        for k in range(slots // 2):
+            second = roll(packed[2 * k + 1], 1)
+            low[k] = jnp.where(even, packed[2 * k], second)
+            high[k] = jnp.where(even, second, packed[2 * k])
+
     def first_faces():
-        for tile in range(slots):
-            for h, value in ((part, field[0, core, tile]), (rest, extra[tile])):
-                packed = pack(columns_of(value))
-                y_first[h, tile] = packed
+        for h in (part, rest):
+            packed = []
+            for tile in range(slots):
+                value = field[0, core, tile] if h is part else extra[tile]
+                packed.append(pack(columns_of(value)))
                 z_first_low[h, tile : tile + 1, :] = value[:1]
                 z_first_high[h, tile : tile + 1, :] = value[half - 1 :]
                 if h is part:
-                    y_here[core, tile] = packed
+                    y_here[core, tile] = packed[tile]
+            in_pairs(packed, y_first_low.at[h], y_first_high.at[h])
 
     def other_faces(tile, carry):
         y_here[other, tile] = pack(columns_of(field[0, other, tile]))
@@ -324,6 +333,14 @@
             even, roll(from_front, 1 - EY - shift), roll(from_back, EY - 1 - shift)
         )
 
+    def paired_ghost(rate, front, back):
+        sides = []
+        for (ok, slot, here, own, other_block), shift in ((front, 1 - EY), (back, EY - 1)):
+            base = jnp.where(ok, jnp.where(here, own, other_block), zero)
+            second = jnp.logical_and(jnp.logical_not(here), lax.rem(slot, 2) == 1)
+            sides.append(jnp.where(second, roll(base, shift - 1), roll(base, shift)))
+        return rate * jnp.where(even, sides[0], sides[1])
+
     def compact(step):
         into = DONE[step + 1]
         later = (step + 1) % 2
@@ -340,36 +357,44 @@
             upper_ok = jnp.where(first, filled, upper_ok)
             for species in range(2):
                 rate = diffusion[species]
-                if step == 0:
-                    shift = 0
-                    from_front = jnp.where(
-                        front_here, y_here[species, front], y_minus[0][species, front])
-                    from_back = jnp.where(
-                        back_here, y_here[species, back], y_plus[0][species, back])
-                elif step == 1:
+                if step == 1:
                     shift = species
                     from_front = jnp.where(front_here, y_high[step, front], y_minus[step][front])
                     from_back = jnp.where(back_here, y_low[step, back], y_plus[step][back])
+                elif step == 2:
+                    shift = species
+                    from_front = jnp.where(
+                        front_here, y_high[DONE[step], front], y_minus[step][front] + g_front[tile])
+                    from_back = jnp.where(
+                        back_here, y_low[DONE[step], back], y_plus[step][back] + g_back[tile])
+                if step == 0:
+                    y_ghost[species, tile] = paired_ghost(
+                        rate,
+                        (front_ok, front, front_here, y_here[species, front],
+                         y_minus[0][species, front // 2]),
+                        (back_ok, back, back_here, y_here[species, back],
+                         y_plus[0][species, back // 2]))
                 else:
-                    shift = species
-                    from_front = jnp.where(front_here, y_high[DONE[step], front], g_front[tile])
-                    from_back = jnp.where(back_here, y_low[DONE[step], back], g_back[tile])
-                from_front = jnp.where(front_ok, from_front, zero)
-                from_back = jnp.where(back_ok, from_back, zero)
-                y_ghost[species, tile] = ghost_of(rate, from_front, from_back, shift)
+                    from_front = jnp.where(front_ok, from_front, zero)
+                    from_back = jnp.where(back_ok, from_back, zero)
+                    y_ghost[species, tile] = ghost_of(rate, from_front, from_back, shift)
                 at = slice(tile, tile + 1)
                 if step < 2:
                     below = pick(lower_ok, z_minus[step], species, pl.ds(lower, 1), slice(None))
                     above = pick(upper_ok, z_plus[step], species, pl.ds(upper, 1), slice(None))
                 else:
-                    below = pick(lower_ok, g_below, species, at, slice(None))
-                    above = pick(upper_ok, g_above, species, at, slice(None))
+                    below = z_minus[step][species, pl.ds(lower, 1), :] + g_below[species, at, :]
+                    above = z_plus[step][species, pl.ds(upper, 1), :] + g_above[species, at, :]
+                    below = jnp.where(lower_ok, below, zero)
+                    above = jnp.where(upper_ok, above, zero)
                 below = rate * below
                 above = rate * above
                 z_ghost_low[species, at, :] = below
                 z_ghost_high[species, at, :] = above
-                z_low[into, species, at, :] = field[later, species, tile, :1, :] + below
-                z_high[into, species, at, :] = field[later, species, tile, half - 1 :, :] + above
+                if step != 1:
+                    z_low[into, species, at, :] = field[later, species, tile, :1, :] + below
+                    z_high[into, species, at, :] = (
+                        field[later, species, tile, half - 1 :, :] + above)
         packed = []
         for species in range(2):
             ghosts = [y_ghost[species, tile] for tile in range(slots)]
@@ -383,20 +408,24 @@
                 high = roll(z_ghost_high[species, :, at], 2 * (top + j))
                 pack_low = jnp.where(row_pair == j, low, pack_low)
                 pack_high = jnp.where(row_pair == top + j, high, pack_high)
-                z_low[into, species, :, at] += jnp.where(row_edge, roll(edge_low, -2 * j), zero)
-                z_high[into, species, :, at] += jnp.where(
-                    row_edge, roll(edge_high, -2 * (top + j)), zero)
+                if step != 1:
+                    z_low[into, species, :, at] += jnp.where(
+                        row_edge, roll(edge_low, -2 * j), zero)
+                    z_high[into, species, :, at] += jnp.where(
+                        row_edge, roll(edge_high, -2 * (top + j)), zero)
             packed.append([
                 y_part[species, tile] + ghosts[tile]
                 + jnp.where(in_low, jnp.broadcast_to(pack_low[tile : tile + 1], (ROWS, LANES)), zero)
                 + jnp.where(in_high, jnp.broadcast_to(pack_high[tile : tile + 1], (ROWS, LANES)), zero)
                 for tile in range(slots)
             ])
-        for tile in range(slots):
-            if step + 1 == STEPS - 1:
-                for species in range(2):
+        if step + 1 == STEPS - 1:
+            for species in range(2):
+                for tile in range(slots):
                     y_last[species, tile] = packed[species][tile]
-            else:
+                in_pairs(packed[species], y_last_low.at[species], y_last_high.at[species])
+        else:
+            for tile in range(slots):
                 second = roll(packed[1][tile], 1)
                 y_low[into, tile] = jnp.where(even, packed[0][tile], second)
                 y_high[into, tile] = jnp.where(even, second, packed[0][tile])
@@ -487,6 +516,16 @@
                 z_high[into, species, :, at] += jnp.where(
                     row_edge, roll(edge, -2 * (top + j)), zero)
 
+    def own_terms(step):
+        low_even_rate = jnp.where(even, diffusion[0], diffusion[1])
+        high_even_rate = jnp.where(even, diffusion[1], diffusion[0])
+        for tile in range(slots):
+            g_front[tile] = high_even_rate * roll(y_low[step, tile], EY - 1)
+            g_back[tile] = low_even_rate * roll(y_high[step, tile], 1 - EY)
+        for species in range(2):
+            g_below[species] = diffusion[species] * z_low[step, species]
+            g_above[species] = diffusion[species] * z_high[step, species]
+
     def complete(step):
         first = part == 0
         both = jnp.logical_and
@@ -521,25 +560,8 @@
                 low = jnp.where(both(sub == 0, form < columns), low, zero)
                 return low + jnp.where(both(sub == ROWS - 1, form >= top), high, zero)
 
-            g_front[tile] = jnp.where(
-                front_cross,
-                y_minus[step + 1][front] + high_even_rate * (
-                    roll(y_low[step, tile], EY - 1) + placed(near_f, side_f, pair_of)),
-                zero)
-            g_back[tile] = jnp.where(
-                back_cross,
-                y_plus[step + 1][back] + low_even_rate * (
-                    roll(y_high[step, tile], 1 - EY) + placed(near_b, side_b, in_low_format)),
-                zero)
-            lower = jnp.where(first, lower, tile)
-            upper = jnp.where(first, tile, upper)
-            for species in range(2):
-                rate = diffusion[species]
-                at = slice(tile, tile + 1)
-                g_below[species, at, :] = (
-                    z_minus[step + 1][species, pl.ds(lower, 1), :] + rate * z_low[step, species, at, :])
-                g_above[species, at, :] = (
-                    z_plus[step + 1][species, pl.ds(upper, 1), :] + rate * z_high[step, species, at, :])
+            g_front[tile] += high_even_rate * placed(near_f, side_f, pair_of)
+            g_back[tile] += low_even_rate * placed(near_b, side_b, in_low_format)
         below_front, below_back = rows_of(below_front), rows_of(below_back)
         above_front, above_back = rows_of(above_front), rows_of(above_back)
         for species in range(2):
@@ -609,16 +631,20 @@
         for s in range(2):
             target = core * 0 + s
             result += [
+                (has_plus, last_copy(
+                    y_last_high.at[s], y_last_minus.at[part], 2 + s, 2 + part,
+                    {"row": band + 1, "pair": target})),
+                (has_minus, last_copy(
+                    y_last_low.at[s], y_last_plus.at[part], 4 + s, 4 + part,
+                    {"row": band - 1, "pair": target})),
+            ]
+        for s in range(2):
+            target = core * 0 + s
+            result += [
                 (both(part == 0, has_down), last_copy(
                     z_low.at[end, s], z_last_plus, s, 0, {"cube": layer - 1, "pair": target})),
                 (both(part == 1, has_up), last_copy(
                     z_high.at[end, s], z_last_minus, s, 1, {"cube": layer + 1, "pair": target})),
-                (has_plus, last_copy(
-                    y_last.at[s], y_last_minus.at[part], 2 + s, 2 + part,
-                    {"row": band + 1, "pair": target})),
-                (has_minus, last_copy(
-                    y_last.at[s], y_last_plus.at[part], 4 + s, 4 + part,
-                    {"row": band - 1, "pair": target})),
             ]
         return result + [
             (always, last_copy(y_last.at[other], y_last_here, 6, 6, partner_id)),
@@ -658,10 +684,10 @@
                     front_in, back_in = y_last_here[front], y_last_here[back]
                     below = rate * jnp.where(first, mine, bottom)
                     above = rate * jnp.where(first, ceiling, mine)
-                from_front = jnp.where(front_here, front_in, y_last_minus[h, front])
-                from_back = jnp.where(back_here, back_in, y_last_plus[h, back])
-                ghost = ghost_of(
-                    rate, jnp.where(front_ok, from_front, zero), jnp.where(back_ok, from_back, zero), 0)
+                ghost = paired_ghost(
+                    rate,
+                    (front_ok, front, front_here, front_in, y_last_minus[h, front // 2]),
+                    (back_ok, back, back_here, back_in, y_last_plus[h, back // 2]))
                 for j in range(columns):
                     lanes = slice(j * LANES, (j + 1) * LANES)
                     if h is part:
@@ -688,22 +714,23 @@
     inner_step(0)
     wait_first()
     compact(0)
+    make_lines()
+    for sent, _, copy in line_messages()[::-1]:
+        pl.when(sent)(copy.start)
     send_faces(1)
-    make_lines()
-    for sent, _, copy in line_messages():
-        pl.when(sent)(copy.start)
     outer_step(0)
     inner_step(1)
     partial_faces(1)
     send_faces(2)
+    own_terms(1)
     wait_faces(1)
     compact(1)
     outer_step(1)
     inner_step(2)
-    wait_faces(2)
     for _, received, copy in line_messages():
         pl.when(received)(copy.wait_recv)
     complete(1)
+    wait_faces(2)
     compact(2)
     for wanted, copy in last_sends():
         pl.when(wanted)(copy.start)
@@ -731,6 +758,7 @@
     _, slots, depth, cells = ligand.shape
     half = depth // 2
     faces = (slots, ROWS, LANES)
+    pairs = (slots // 2, ROWS, LANES)
     planes = (2, slots, cells)
     away = pl.BlockSpec(memory_space=pltpu.HBM)
     neighbours, diffusion, uptake = [
@@ -746,14 +774,15 @@
             pltpu.VMEM((slots, half, cells), jnp.int32),
             pltpu.VMEM((STEPS + 1,) + faces, jnp.float32),
             pltpu.VMEM((STEPS + 1,) + faces, jnp.float32),
-            [pltpu.VMEM((2,) + faces, jnp.float32)] + [pltpu.VMEM(faces, jnp.float32)] * (STEPS - 2),
-            [pltpu.VMEM((2,) + faces, jnp.float32)] + [pltpu.VMEM(faces, jnp.float32)] * (STEPS - 2),
+            [pltpu.VMEM((2,) + pairs, jnp.float32)] + [pltpu.VMEM(faces, jnp.float32)] * (STEPS - 2),
+            [pltpu.VMEM((2,) + pairs, jnp.float32)] + [pltpu.VMEM(faces, jnp.float32)] * (STEPS - 2),
             pltpu.VMEM((STEPS + 1,) + planes, jnp.float32),
             pltpu.VMEM((STEPS + 1,) + planes, jnp.float32),
             [pltpu.VMEM(planes, jnp.float32)] * (STEPS - 1),
             [pltpu.VMEM(planes, jnp.float32)] * (STEPS - 1),
             pltpu.VMEM((slots, half, cells), jnp.float32),
-            pltpu.VMEM((2,) + faces, jnp.float32),
+            pltpu.VMEM((2,) + pairs, jnp.float32),
+            pltpu.VMEM((2,) + pairs, jnp.float32),
             pltpu.VMEM((2,) + faces, jnp.float32),
             pltpu.VMEM(planes, jnp.float32),
             pltpu.VMEM(planes, jnp.float32),
@@ -762,9 +791,11 @@
             pltpu.VMEM(planes, jnp.float32),
             pltpu.VMEM(planes, jnp.float32),
             pltpu.VMEM((2,) + faces, jnp.float32),
+            pltpu.VMEM((2,) + pairs, jnp.float32),
+            pltpu.VMEM((2,) + pairs, jnp.float32),
             pltpu.VMEM(faces, jnp.float32),
-            pltpu.VMEM((2,) + faces, jnp.float32),
-            pltpu.VMEM((2,) + faces, jnp.float32),
+            pltpu.VMEM((2,) + pairs, jnp.float32),
+            pltpu.VMEM((2,) + pairs, jnp.float32),
             pltpu.VMEM((slots, cells), jnp.float32),
             pltpu.VMEM((slots, cells), jnp.float32),
             pltpu.VMEM((slots, cells), jnp.float32),

time: 16.5 us -> 16.4 us (level)
  no operation moved by 1% of the time
where the time goes in v4:
time: 16.4 us; the launch traced here: 16.3 us
  Pallas kernels  14.8 us (90%)
  local copies, waits for them, and re-layouts  0.8 us (5%)
  between operations  0.66 us (4%)
    pallas_call x1, Pallas kernels, per_device(): pl.pallas_call(functools.partial(kernel, layers, bands, slots, half, cell...  14.8 us
    unnamed x1, local copies, waits for them, and re-layouts  0.8 us

profile of v4, /device:TPU:0, one launch (start us, length us, event | category | flops | bytes accessed | tf_op | source)
XLA Modules:
  0.0 16.3 jit_solution(14998245668780218016)
XLA Ops:
  0.7 14.8 %shard_map.64 = f32[1,4,32,1024]{3,2,1,0:T(8,128)S(1)} custom-call(s32[4,6]{1,0:T(4,128)} %nbr_in.1, s32[1]{0:T(128)S(6)} %copy.8.counts_in, f32[2]{0:T(128)} %diffusion_in.1, f32[2]{0:T(128)} %uptake_in.1, f32[1,4,32,1024]{3,2,1,0:T(8,128)} %ligand.1, s32[4,32,1024]{2,1,0:T(8,128)} %density.1), custom_call_target="tpu_custom_call" | custom-call | tf_op jit(solution)/shard_map/pallas_call | solution.py:767
  15.5 0.8 %copy.9 = f32[1,4,32,1024]{3,2,1,0:T(8,128)} copy(f32[1,4,32,1024]{3,2,1,0:T(8,128)S(1)} %shard_map.64) | data formatting | bytes 1048576
